TPU v7x, 256 devices: a whole 4x4x8 slice. The times are simulated.
256 devices in a mesh: seq: 32 (over z, x), res: 8 (over y, core).
Axes of the slice: x: 4, y: 4, z: 8, core: 2. Of those that a mesh axis runs over, the one named last changes fastest.
Arguments:
- alignment_rows: float32 [128, 1024, 768], P('seq', 'res'), may hold values from -5 to 5
- query_matrix: bfloat16 [768, 768], replicated, may hold values from -1 to 1
- key_matrix: bfloat16 [768, 768], replicated, may hold values from -1 to 1
- value_matrix: bfloat16 [768, 768], replicated, may hold values from -0.21875 to 0.21875
- output_matrix: bfloat16 [768, 768], replicated, may hold values from -1.5 to 1.5
Outputs:
- attended_rows: float32 [128, 1024, 768], P('seq', 'res')
All inputs are finite; a program needn't handle non-finite values.
Results may differ from a plain program's by a relative error of at most 0.012.
Values may be sent and summed in bfloat16 or wider, within the bound.
A program may use at most 128 MiB of HBM per device.

v0:
```python
import math

import jax
import jax.numpy as jnp
from jax import lax
from jax.sharding import PartitionSpec as P

HEADS = 12
HEAD_DIM = 64


epsilon = 1e-05


def layer_normalize(values):
    mean_val = jnp.mean(values, axis=-1, keepdims=True)
    centred = values - mean_val
    spread = jnp.mean(centred * centred, axis=-1, keepdims=True)
    return centred * lax.rsqrt(spread + epsilon)


def body(alignment_rows, query_matrix, key_matrix, value_matrix, output_matrix):
    sequence_local_count, residue_local_count, hidden_width = alignment_rows.shape
    seq_count = lax.axis_size("seq")
    normalized_rows = (
        layer_normalize(alignment_rows)
        .astype(jnp.bfloat16)
        .reshape(sequence_local_count * residue_local_count, hidden_width)
    )

    def project(weight):
        full = jnp.dot(normalized_rows, weight, preferred_element_type=jnp.float32).astype(
            jnp.bfloat16
        )
        return full.reshape(sequence_local_count, residue_local_count, HEADS, HEAD_DIM)

    queries = project(query_matrix)
    keys_own = project(key_matrix)
    values_own = project(value_matrix)
    scale_val = 1.0 / math.sqrt(HEAD_DIM * sequence_local_count * seq_count)
    partial_scores = jnp.einsum(
        "sihd,sjhd->hij",
        queries,
        lax.all_gather(keys_own, "res", axis=1, tiled=True),
        preferred_element_type=jnp.float32,
    )
    summed_scores = lax.psum(partial_scores, "seq") * scale_val
    peak_val = jnp.max(summed_scores, axis=2, keepdims=True)
    expo = jnp.exp(summed_scores - peak_val)
    weights_bf = (expo / jnp.sum(expo, axis=2, keepdims=True)).astype(jnp.bfloat16)
    mixed_all = jnp.einsum(
        "hij,sjhd->sihd",
        weights_bf,
        lax.all_gather(values_own, "res", axis=1, tiled=True),
        preferred_element_type=jnp.float32,
    )
    mixed = mixed_all.astype(jnp.bfloat16).reshape(
        sequence_local_count * residue_local_count, hidden_width
    )
    result = jnp.dot(mixed, output_matrix, preferred_element_type=jnp.float32)
    return result.reshape(sequence_local_count, residue_local_count, hidden_width)


def solution(mesh):
    in_specs = (P("seq", "res", None), P(), P(), P(), P())
    out_specs = P("seq", "res", None)
    return jax.shard_map(body, mesh=mesh, in_specs=in_specs, out_specs=out_specs, check_vma=False)
```

profile of v0, /device:TPU:16, one launch (start us, length us, event | category | flops | bytes accessed | tf_op | source)
XLA Modules:
  0.0 321.8 jit_solution(3938439028467260270)
XLA Ops:
  6.5 0.0 copy-start
  6.5 0.0 all-gather.5.cloned.1.call-start
  6.5 1.7 reduce_sum.27
  8.2 1.7 multiply_reduce_fusion.1
  9.9 1.6 multiply_convert_fusion
  11.6 0.0 copy-done
  11.6 0.8 convolution_convert_fusion
  12.4 0.3 copy.12
  12.6 0.2 reshape.33
  12.8 1.1 copy.13
  13.9 0.0 all-gather.5.cloned.1.call-update
  13.9 0.0 all-reduce.2.cloned.1.call-start
  14.0 2.0 convolution_convert_fusion.1
  16.0 0.3 copy.11
  16.3 0.2 reshape.32
  16.5 47.6 %all-gather.5.cloned.1.call-done = bf16[4,1024,12,64]{1,3,0,2:T(8,128)(2,1)} async-done(((bf16[4,128,12,64]{1,3,0,2:T(8,128)(2,1)}), bf16[4,1024,12,64]{1,3,0,2:T(8,128)(2,1)}) %all-gather.5.cloned.1.call-update) | async-done | bytes 6291472 | tf_op jit(solution)/shard_map/all_gather | solution.py:44
  64.1 6.5 %convolution_bitcast_fusion = f32[12,128,1024]{2,1,0:T(8,128)} fusion(bf16[4,1024,12,64]{1,3,0,2:T(8,128)(2,1)} %all-gather.5.cloned.1.call-done, bf16[4,128,12,64]{1,0,3,2:T(4,128)(2,1)S(1)} %reshape.32), kind=kOutput, calls=%fused_computation.8 | convolution fusion | flops 805306368 | bytes 13369344 | tf_op jit(solution)/shard_map/sihd,sjhd->hij/dot_general | solution.py:41
  70.6 0.0 all-reduce.2.cloned.1.call-update
  70.6 0.0 all-gather.3.cloned.1.call-start
  70.7 2.0 convolution_convert_fusion.2
  72.7 0.3 copy.9
  73.0 0.2 reshape.31
  73.2 1.1 copy.10
  74.3 0.0 all-gather.3.cloned.1.call-update
  74.3 181.5 %all-reduce.2.cloned.1.call-done = f32[12,128,1024]{2,1,0:T(8,128)} async-done(((f32[12,128,1024]{2,1,0:T(8,128)}), f32[12,128,1024]{2,1,0:T(8,128)}) %all-reduce.2.cloned.1.call-update) | async-done | bytes 6291472 | tf_op jit(solution)/shard_map/psum | solution.py:47
  255.8 6.4 %fusion.24 = f32[12,128]{1,0:T(8,128)S(1)} fusion(f32[12,128,1024]{2,1,0:T(8,128)} %all-reduce.2.cloned.1.call-done), kind=kOutput, calls=%fused_computation.24 | output fusion | flops 6292479 | bytes 6297600 | tf_op jit(solution)/shard_map/sub | solution.py:49
  262.2 0.0 copy-start.1
  262.3 41.5 %all-gather.3.cloned.1.call-done = bf16[4,1024,12,64]{1,3,0,2:T(8,128)(2,1)} async-done(((bf16[4,128,12,64]{1,3,0,2:T(8,128)(2,1)}), bf16[4,1024,12,64]{1,3,0,2:T(8,128)(2,1)}) %all-gather.3.cloned.1.call-update) | async-done | bytes 6291472 | tf_op jit(solution)/shard_map/all_gather | solution.py:54
  303.8 9.5 %fusion.10 = bf16[4,128,12,64]{1,3,0,2:T(8,128)(2,1)S(1)} fusion(bf16[4,1024,12,64]{1,3,0,2:T(8,128)(2,1)} %all-gather.3.cloned.1.call-done, f32[12,128]{1,0:T(8,128)S(1)} %fusion.24, f32[12,128,1024]{2,1,0:T(8,128)} %all-reduce.2.cloned.1.call-done), kind=kOutput, calls=%fused_computation.15 | convolution fusion | flops 813566464 | bytes 13375488 | tf_op jit(solution)/shard_map/hij,sjhd->sihd/dot_general | solution.py:51
  313.2 0.1 copy.15
  313.3 0.0 copy-done.1
  313.3 2.0 fusion.13
  (2 shorter events, 0.0 us)
Async XLA Ops:
  6.5 5.0 %copy-start = (bf16[768,768]{1,0:T(8,128)(2,1)S(1)}, bf16[768,768]{1,0:T(8,128)(2,1)}, u32[]{:S(2)}) copy-start(bf16[768,768]{1,0:T(8,128)(2,1)} %param.7) | copy-start | bytes 3538948
  6.5 57.6 %all-gather.5.cloned.1.call-start = ((), (), s32[]{:S(2)}) async-start(), calls=%async_computation.1 | async-start | bytes 7077888 | tf_op jit(solution)/shard_map/all_gather | solution.py:44
  13.9 241.9 %all-reduce.2.cloned.1.call-start = ((), (), s32[]{:S(2)}) async-start(), calls=%async_computation.2 | async-start | bytes 12582912 | tf_op jit(solution)/shard_map/psum | solution.py:47
  70.6 233.1 %all-gather.3.cloned.1.call-start = ((), (), s32[]{:S(2)}) async-start(), calls=%async_computation | async-start | bytes 7077888 | tf_op jit(solution)/shard_map/all_gather | solution.py:54
  262.2 51.1 %copy-start.1 = (bf16[768,768]{1,0:T(8,128)(2,1)S(1)}, bf16[768,768]{1,0:T(8,128)(2,1)}, u32[]{:S(2)}) copy-start(bf16[768,768]{1,0:T(8,128)(2,1)} %param.9) | copy-start | bytes 3538948
Sparse Core Ops, SparseCore 0:
  14.0 50.0 all-gather.4
  70.8 185.0 all-reduce.1
  257.8 45.9 all-gather.2
where the time goes:
time: 324 us; the launch traced here: 322 us
  waiting for transfers between devices  271 us (84%)
  matrix products  22.8 us (7%)
  between operations  13.2 us (4%)
  other arithmetic  11.4 us (4%)
  local copies, waits for them, and re-layouts  3.59 us (1%)
    psum x1, waiting for transfers between devices, body(): summed_scores = lax.psum(partial_scores, 'seq') * scale_val  182 us
    all_gather x1, waiting for transfers between devices, body(): lax.all_gather(keys_own, 'res', axis=1, tiled=True)  47.6 us
    all_gather x1, waiting for transfers between devices, body(): lax.all_gather(values_own, 'res', axis=1, tiled=True)  41.5 us
    dot_general x1, matrix products, body(): jnp.einsum('hij,sjhd->sihd', weights_bf, lax.all_gather(values_own, 'res'...  9.47 us
    dot_general x1, matrix products, body(): jnp.einsum('sihd,sjhd->hij', queries, lax.all_gather(keys_own, 'res', axi...  6.51 us
  transfers between devices with their start and end apart: 3, of which 3 were waited for; matrix products, arithmetic and copies ran while one was open for 4% of the time, Pallas kernels for 0%

commit v1 on v0

v1 whole, which is shorter than its diff:
```python
import math

import jax
import jax.numpy as jnp
from jax import lax
from jax.experimental import pallas as pl
from jax.experimental.pallas import tpu as pltpu
from jax.sharding import PartitionSpec as P

MESH = pl.DeviceIdType.MESH
F32 = jnp.float32
BF16 = jnp.bfloat16

NZ, NX, NY = 8, 4, 4
CHUNKS = 3
SEQ_LOCAL, RES_LOCAL, WIDTH = 4, 128, 768
ROWS = NY * RES_LOCAL
COLS = 2 * ROWS
DEPTH = 256
SCALE = 1.0 / math.sqrt(64 * 128)
EPSILON = 1e-05
N_SEMS = 128


def kernel(
    x_hbm, wq_hbm, wk_hbm, wv_hbm, wo_hbm, o_ref,
    x_v, n_v, w_v, wo_v, send_v, q_v, k_v, v_v, sc_v, p_v,
    rx1, rxl, rxr, tmp, xs_v, rz, rzr, rzl, tz, zs_v, rx, os_v, ob_v, m_v,
    load_sem, ss, rs,
):
    s_id, r_id = lax.axis_index("seq"), lax.axis_index("res")
    z, x = s_id // NX, s_id % NX
    y, core = r_id // 2, r_id % 2

    def dev(dz=0, dx=0, dy=0, dc=0):
        return (
            ((z + dz) % NZ) * NX + (x + dx) % NX,
            ((y + dy) % NY) * 2 + (core + dc) % 2,
        )

    partners = (
        [dict(dy=d) for d in (1, 2, 3)]
        + [dict(dc=1)]
        + [dict(dx=d) for d in (1, 2, 3)]
        + [dict(dz=d) for d in range(1, 8)]
    )

    loads = {}
    n_load = [0]

    def load(name, src, dst):
        c = pltpu.make_async_copy(src, dst, load_sem.at[n_load[0]])
        n_load[0] += 1
        c.start()
        loads[name] = c

    for s in range(SEQ_LOCAL):
        load(("x", s), x_hbm.at[s], x_v.at[s])
    w_hbm = (wq_hbm, wk_hbm, wv_hbm)
    for t in (0, 1):
        load(("w", t, 0), w_hbm[t].at[:, pl.ds(0, DEPTH)], w_v.at[t, 0])
    for c in (1, 2):
        for t in (0, 1):
            load(("w", t, c), w_hbm[t].at[:, pl.ds(c * DEPTH, DEPTH)], w_v.at[t, c])
    for c in range(CHUNKS):
        load(("w", 2, c), w_hbm[2].at[:, pl.ds(c * DEPTH, DEPTH)], w_v.at[2, c])
    load("wo", wo_hbm, wo_v)

    barrier = pltpu.get_barrier_semaphore()
    for p in partners:
        pl.semaphore_signal(barrier, inc=1, device_id=dev(**p), device_id_type=MESH)

    count = [0]
    started = []

    def send(src, dst, **where):
        i = count[0]
        count[0] += 1
        c = pltpu.make_async_remote_copy(
            src_ref=src, dst_ref=dst, send_sem=ss.at[i], recv_sem=rs.at[i],
            device_id=dev(**where), device_id_type=MESH,
        )
        c.start()
        started.append(c)
        return c

    for s in range(SEQ_LOCAL):
        loads[("x", s)].wait()
        v = x_v[s]
        mean = jnp.mean(v, axis=-1, keepdims=True)
        cen = v - mean
        var = jnp.mean(cen * cen, axis=-1, keepdims=True)
        n_v[pl.ds(s * RES_LOCAL, RES_LOCAL), :] = (cen * lax.rsqrt(var + EPSILON)).astype(BF16)

    def swap(blocks, j):
        return jnp.concatenate([b[:, 64 * j : 64 * j + 64] for b in blocks], axis=1)

    def project(t, c):
        loads[("w", t, c)].wait()
        full = jnp.dot(n_v[...], w_v[t, c], preferred_element_type=F32).astype(BF16)
        blocks = [full[s * RES_LOCAL : (s + 1) * RES_LOCAL] for s in range(SEQ_LOCAL)]
        for j in range(NY):
            send_v[t, c, j] = swap(blocks, j)

    homes = (q_v, None, None)

    def home(t, c):
        if t == 0:
            return q_v.at[c]
        return (k_v if t == 1 else v_v).at[c, 0]

    def send_y(t, c):
        out = []
        for d in (1, 2, 3):
            out.append(send(send_v.at[t, c, (y + d) % NY], home(t, c).at[y], dy=d))
        return out

    def keep(t, c):
        home(t, c)[y] = send_v[t, c, y]

    def core_swap(t, c):
        b = (k_v if t == 1 else v_v)
        return send(b.at[c, 0], b.at[c, 1], dc=1)

    def scores(c):
        q = q_v[c].reshape(ROWS, DEPTH)

        def step(n, carry):
            half, part = n // 2, n % 2
            k = k_v[c, half, pl.ds(part * 2, 2)].reshape(2 * RES_LOCAL, DEPTH)
            r = lax.dot_general(q, k, (((1,), (1,)), ((), ())), preferred_element_type=F32)
            sc_v[c, :, pl.ds(pl.multiple_of(n * 256, 256), 256)] = (r * SCALE).astype(BF16)
            return carry

        lax.fori_loop(0, 4, step, 0)

    def rows(ref, off, n):
        return ref[pl.ds(pl.multiple_of(off, 16), n), :].astype(F32)

    def at(ref, off, n):
        return ref.at[pl.ds(pl.multiple_of(off, 16), n)]

    xr, xl, xo = (x + 1) % NX, (x + 3) % NX, (x + 2) % NX

    def softmax16(v):
        peak = jnp.max(v, axis=-1, keepdims=True)
        e = jnp.exp(v - peak)
        return (e / jnp.sum(e, axis=-1, keepdims=True)).astype(BF16)

    def xfirst(c, g):
        sc = sc_v.at[c]
        pv = p_v.at[c]
        st = {}

        def start():
            st["r1"] = send(at(sc, xo * 128, 64), rx1.at[g, 0], dx=1)
            st["l1"] = send(at(sc, xo * 128 + 64, 64), rx1.at[g, 1], dx=3)
            st["r2"] = send(at(sc, xr * 128 + 64, 64), rxl.at[g, pl.ds(64, 64)], dx=1)
            st["l2"] = send(at(sc, xl * 128, 64), rxr.at[g, pl.ds(0, 64)], dx=3)

        def relay():
            st["r1"].wait_recv()
            tmp[g, 0] = (rows(sc, xr * 128, 64) + rx1[g, 0].astype(F32)).astype(BF16)
            st["r3"] = send(tmp.at[g, 0], rxl.at[g, pl.ds(0, 64)], dx=1)
            st["l1"].wait_recv()
            tmp[g, 1] = (rows(sc, xl * 128 + 64, 64) + rx1[g, 1].astype(F32)).astype(BF16)
            st["l3"] = send(tmp.at[g, 1], rxr.at[g, pl.ds(64, 64)], dx=3)

        def zsend():
            for k in ("r2", "l2", "r3", "l3"):
                st[k].wait_recv()
            total = rows(sc, x * 128, 128) + rxl[g].astype(F32) + rxr[g].astype(F32)
            xs_v[g] = total.astype(BF16).reshape(NZ, 16, COLS)
            st["z"] = [
                send(xs_v.at[g, (z + d) % NZ], rz.at[g, d - 1], dz=d) for d in range(1, 8)
            ]

        def finish():
            own = z * 16
            total = rows(sc, x * 128 + own, 16)
            total = total + rows(rxl.at[g], own, 16) + rows(rxr.at[g], own, 16)
            for d in range(7):
                st["z"][d].wait_recv()
                total = total + rz[g, d].astype(F32)
            mine = at(pv, x * 128 + own, 16)
            mine[...] = softmax16(total)
            st["za"] = [send(mine, mine, dz=d) for d in range(1, 8)]

        def xgather():
            for k in st["za"]:
                k.wait_recv()
            block = at(pv, x * 128, 128)
            st["ra"] = send(block, block, dx=1)
            st["la"] = send(block, block, dx=3)

        def xforward():
            st["ra"].wait_recv()
            block = at(pv, xl * 128, 64)
            st["rb"] = send(block, block, dx=1)
            st["la"].wait_recv()
            block = at(pv, xr * 128 + 64, 64)
            st["lb"] = send(block, block, dx=3)

        def done():
            st["rb"].wait_recv()
            st["lb"].wait_recv()

        return [start, relay, zsend, finish, xgather, xforward, done]

    def zfirst(c):
        sc = sc_v.at[c]
        pv = p_v.at[c]
        st = {}

        def ring(k):
            def go():
                if k == 1:
                    st["r"] = send(at(sc, ((z + 4) % NZ) * 64, 32), rzr.at[0, pl.ds(0, 32)], dz=1)
                    st["l"] = send(at(sc, ((z + 4) % NZ) * 64 + 32, 32), rzl.at[0, pl.ds(32, 32)], dz=7)
                    return
                dr, dl = (z + 5 - k) % NZ, (z + 3 + k) % NZ
                st["r"].wait_recv()
                if k == 2:
                    tz[0, 0, pl.ds(0, 32), :] = (
                        rows(sc, dr * 64, 32) + rzr[0, pl.ds(0, 32), :].astype(F32)
                    ).astype(BF16)
                    tz[0, 0, pl.ds(32, 32), :] = sc[pl.ds(pl.multiple_of(dr * 64 + 32, 32), 32), :]
                else:
                    tz[k - 2, 0] = (rows(sc, dr * 64, 64) + rzr[k - 2].astype(F32)).astype(BF16)
                st["r"] = send(tz.at[k - 2, 0], rzr.at[k - 1], dz=1)
                st["l"].wait_recv()
                if k == 2:
                    tz[0, 1, pl.ds(32, 32), :] = (
                        rows(sc, dl * 64 + 32, 32) + rzl[0, pl.ds(32, 32), :].astype(F32)
                    ).astype(BF16)
                    tz[0, 1, pl.ds(0, 32), :] = sc[pl.ds(pl.multiple_of(dl * 64, 32), 32), :]
                else:
                    tz[k - 2, 1] = (rows(sc, dl * 64, 64) + rzl[k - 2].astype(F32)).astype(BF16)
                st["l"] = send(tz.at[k - 2, 1], rzl.at[k - 1], dz=7)

            return go

        def xsend():
            st["r"].wait_recv()
            st["l"].wait_recv()
            zs_v[...] = (
                rows(sc, z * 64, 64) + rzr[3].astype(F32) + rzl[3].astype(F32)
            ).reshape(NX, 16, COLS)
            st["x"] = [send(zs_v.at[(x + d) % NX], rx.at[d - 1], dx=d) for d in (1, 2, 3)]

        def finish():
            total = zs_v[x]
            for d in range(3):
                st["x"][d].wait_recv()
                total = total + rx[d]
            mine = at(pv, z * 64 + x * 16, 16)
            mine[...] = softmax16(total)
            st["xa"] = [send(mine, mine, dx=d) for d in (1, 2, 3)]

        def gather(k):
            def go():
                if k == 1:
                    for cp in st["xa"]:
                        cp.wait_recv()
                    b = at(pv, z * 64, 64)
                    st["gr"] = send(b, b, dz=1)
                    st["gl"] = send(b, b, dz=7)
                    return
                zr, zl = (z + k - 1) % NZ, (z + 9 - k) % NZ
                st["gr"].wait_recv()
                b = at(pv, zl * 64, 64 if k < 4 else 32)
                st["gr"] = send(b, b, dz=1)
                st["gl"].wait_recv()
                b = at(pv, zr * 64, 64) if k < 4 else at(pv, zr * 64 + 32, 32)
                st["gl"] = send(b, b, dz=7)

            return go

        def done():
            st["gr"].wait_recv()
            st["gl"].wait_recv()

        return [ring(1), ring(2), ring(3), ring(4), xsend, finish, gather(1), gather(2), gather(3), gather(4), done]

    def mix(c):
        v = v_v[c].reshape(COLS, DEPTH)

        def step(i, carry):
            m = jnp.dot(
                p_v[c, pl.ds(pl.multiple_of(i * 256, 256), 256), :], v, preferred_element_type=F32
            ).astype(BF16)
            os_v[c, pl.ds(i * 2, 2)] = m.reshape(2, RES_LOCAL, DEPTH)
            return carry

        lax.fori_loop(0, 2, step, 0)
        ob_v[c, y] = os_v[c, y]
        return [send(os_v.at[c, (y + d) % NY], ob_v.at[c, y], dy=d) for d in (1, 2, 3)]

    def output(c, first):
        blocks = [ob_v[c, j] for j in range(NY)]
        for s in range(SEQ_LOCAL):
            m_v[pl.ds(s * RES_LOCAL, RES_LOCAL), :] = swap(blocks, s)

        def step(n, carry):
            cols = pl.ds(pl.multiple_of(n * 256, 256), 256)
            r = jnp.dot(
                m_v[...], wo_v[pl.ds(c * DEPTH, DEPTH), cols], preferred_element_type=F32
            )
            if first:
                o_ref[:, cols] = r
            else:
                o_ref[:, cols] += r
            return carry

        lax.fori_loop(0, 3, step, 0)

    def wait_all(cps):
        for cp in cps:
            cp.wait_recv()

    project(0, 0)
    project(1, 0)
    pl.semaphore_wait(barrier, len(partners))
    qk = {}
    qk[0] = send_y(1, 0) + send_y(0, 0)
    keep(0, 0), keep(1, 0)
    for c in (1, 2):
        project(0, c), project(1, c)
        keep(0, c), keep(1, c)
    h0 = xfirst(0, 0)
    h1 = zfirst(1)
    h2 = xfirst(2, 1)

    def take(c):
        wait_all(qk[c][:3])
        kc = core_swap(1, c)
        wait_all(qk[c][3:])
        if c < 2:
            qk[c + 1] = send_y(1, c + 1) + send_y(0, c + 1)
        kc.wait_recv()
        scores(c)

    take(0)
    h0[0]()
    for c in range(CHUNKS):
        project(2, c)
        keep(2, c)
    h0[1]()
    take(1)
    h1[0]()
    h1[1]()
    h0[2]()
    h1[2]()
    take(2)
    vs = [send_y(2, c) for c in range(CHUNKS)]
    h2[0]()
    h1[3]()
    h2[1]()
    h0[3]()
    h1[4]()
    h2[2]()
    h0[4]()
    h1[5]()
    h1[6]()
    h2[3]()
    h0[5]()
    h1[7]()
    vc = []
    for c in range(CHUNKS):
        wait_all(vs[c])
        vc.append(core_swap(2, c))
    h2[4]()
    h1[8]()
    h1[9]()
    loads["wo"].wait()
    h0[6]()
    vc[0].wait_recv()
    o0 = mix(0)
    h2[5]()
    h1[10]()
    vc[1].wait_recv()
    o1 = mix(1)
    wait_all(o0)
    output(0, True)
    wait_all(o1)
    output(1, False)
    h2[6]()
    vc[2].wait_recv()
    o2 = mix(2)
    wait_all(o2)
    output(2, False)
    for cp in started:
        cp.wait_send()


def body(alignment_rows, query_matrix, key_matrix, value_matrix, output_matrix):
    any_spec = pl.BlockSpec(memory_space=pl.ANY)
    V = pltpu.VMEM
    out = pl.pallas_call(
        kernel,
        out_shape=jax.ShapeDtypeStruct((SEQ_LOCAL * RES_LOCAL, WIDTH), F32),
        in_specs=[any_spec] * 5,
        out_specs=pl.BlockSpec(memory_space=V),
        scratch_shapes=[
            V((SEQ_LOCAL, RES_LOCAL, WIDTH), F32),
            V((SEQ_LOCAL * RES_LOCAL, WIDTH), BF16),
            V((3, CHUNKS, WIDTH, DEPTH), BF16),
            V((WIDTH, WIDTH), BF16),
            V((3, CHUNKS, NY, RES_LOCAL, DEPTH), BF16),
            V((CHUNKS, NY, RES_LOCAL, DEPTH), BF16),
            V((CHUNKS, 2, NY, RES_LOCAL, DEPTH), BF16),
            V((CHUNKS, 2, NY, RES_LOCAL, DEPTH), BF16),
            V((CHUNKS, ROWS, COLS), BF16),
            V((CHUNKS, ROWS, COLS), BF16),
            V((2, 2, 64, COLS), BF16),
            V((2, 128, COLS), BF16),
            V((2, 128, COLS), BF16),
            V((2, 2, 64, COLS), BF16),
            V((2, NZ, 16, COLS), BF16),
            V((2, 7, 16, COLS), BF16),
            V((4, 64, COLS), BF16),
            V((4, 64, COLS), BF16),
            V((3, 2, 64, COLS), BF16),
            V((NX, 16, COLS), F32),
            V((3, 16, COLS), F32),
            V((CHUNKS, NY, RES_LOCAL, DEPTH), BF16),
            V((CHUNKS, NY, RES_LOCAL, DEPTH), BF16),
            V((SEQ_LOCAL * RES_LOCAL, DEPTH), BF16),
            pltpu.SemaphoreType.DMA((16,)),
            pltpu.SemaphoreType.DMA((N_SEMS,)),
            pltpu.SemaphoreType.DMA((N_SEMS,)),
        ],
        compiler_params=pltpu.CompilerParams(
            collective_id=0, has_side_effects=True, vmem_limit_bytes=56 << 20
        ),
        cost_estimate=pl.CostEstimate(
            flops=9_000_000_000, bytes_accessed=8_000_000, transcendentals=60_000
        ),
    )(alignment_rows, query_matrix, key_matrix, value_matrix, output_matrix)
    return out.reshape(alignment_rows.shape)


def solution(mesh):
    in_specs = (P("seq", "res", None), P(), P(), P(), P())
    out_specs = P("seq", "res", None)
    return jax.shard_map(body, mesh=mesh, in_specs=in_specs, out_specs=out_specs, check_vma=False)
```

time: 324 us -> 104 us (0.32)
  waiting for transfers between devices: 271 us -> 0 us
  Pallas kernels: 0 us -> 99.7 us
  matrix products: 22.8 us -> 0 us
  between operations: 13.2 us -> 0.01 us
  other arithmetic: 11.4 us -> 0 us
    psum x1 -> x0, waiting for transfers between devices: 182 us -> none  [body(): summed_scores = lax.psum(partial_scores, 'seq') * scale_val]
    pallas_call x0 -> x1, Pallas kernels: none -> 99.7 us  [body(): pl.pallas_call(kernel, out_shape=jax.ShapeDtypeStruct((SEQ_LOCAL * RES_LO...]
    all_gather x2 -> x0, waiting for transfers between devices: 89.1 us -> none  [the longest x1 47.6 us: body(): lax.all_gather(keys_own, 'res', axis=1, tiled=True)]
    dot_general x6 -> x0, matrix products: 22.8 us -> none  [the longest x1 9.47 us: body(): jnp.einsum('hij,sjhd->sihd', weights_bf, lax.all_gather(values_own, 'res'...]
    sub x1 -> x0, other arithmetic: 6.41 us -> none  [body(): expo = jnp.exp(summed_scores - peak_val)]
    reduce_sum x2 -> x0, other arithmetic: 3.36 us -> none  [the longest x1 1.7 us: layer_normalize(): spread = jnp.mean(centred * centred, axis=-1, keepdims=True)]
  transfers between devices with their start and end apart: 3 -> 0, of which waited for: 3 -> 0; matrix products, arithmetic and copies ran while one was open for 4% -> 0% of each run, Pallas kernels for 0% -> 0%
where the time goes in v1:
time: 104 us; the launch traced here: 102 us
  Pallas kernels  99.7 us (96%)
  local copies, waits for them, and re-layouts  2.69 us (3%)
    pallas_call x1, Pallas kernels, body(): pl.pallas_call(kernel, out_shape=jax.ShapeDtypeStruct((SEQ_LOCAL * RES_LO...  99.7 us
    unnamed x1, local copies, waits for them, and re-layouts  2.69 us

profile of v1, /device:TPU:16, one launch (start us, length us, event | category | flops | bytes accessed | tf_op | source)
XLA Modules:
  0.0 102.5 jit_solution(11356447636257191785)
XLA Ops:
  0.0 99.7 %shard_map.55 = f32[512,768]{1,0:T(8,128)} custom-call(f32[4,128,768]{2,1,0:T(8,128)} %x_hbm.1, bf16[768,768]{1,0:T(8,128)(2,1)} %wq_hbm.1, bf16[768,768]{1,0:T(8,128)(2,1)} %wk_hbm.1, bf16[768,768]{1,0:T(8,128)(2,1)} %wv_hbm.1, bf16[768,768]{1,0:T(8,128)(2,1)} %wo_hbm.1), custom_call_target="tpu_custom_call" | custom-call | flops 8999999488 | bytes 8000000 | tf_op jit(solution)/shard_map/pallas_call | solution.py:399
  99.8 2.7 %copy.7 = f32[4,128,768]{2,1,0:T(8,128)} copy(f32[4,128,768]{2,1,0:T(8,128)} %bitcast.1) | data formatting | bytes 3145728

commit v2 on v0

v2 whole, which is shorter than its diff:
```python
import math

import jax
import jax.numpy as jnp
from jax import lax
from jax.experimental import pallas as pl
from jax.experimental.pallas import tpu as pltpu
from jax.sharding import PartitionSpec as P

MESH = pl.DeviceIdType.MESH
F32 = jnp.float32
BF16 = jnp.bfloat16

NZ, NX, NY = 8, 4, 4
CHUNKS = 3
SEQ_LOCAL, RES_LOCAL, WIDTH = 4, 128, 768
ROWS = NY * RES_LOCAL
COLS = 2 * ROWS
DEPTH = 256
SCALE = 1.0 / math.sqrt(64 * 128)
EPSILON = 1e-05
N_SEMS = 216

GROUPS = (("x", 768), ("z", 256),)


def kernel(x_hbm, wq_hbm, wk_hbm, wv_hbm, o_ref, *scratch):
    (x_v, n_v, w_v, send_v, q_v, k_v, v_v, os_v, ob_v, m_v, load_sem, ss, rs) = scratch[:13]
    group_refs, at = [], 13
    for kind, _ in GROUPS:
        size = 8 if kind == "x" else 7
        group_refs.append(scratch[at : at + size])
        at += size
    s_id, r_id = lax.axis_index("seq"), lax.axis_index("res")
    z, x = s_id // NX, s_id % NX
    y, core = r_id // 2, r_id % 2

    def dev(dz=0, dx=0, dy=0, dc=0):
        return (
            ((z + dz) % NZ) * NX + (x + dx) % NX,
            ((y + dy) % NY) * 2 + (core + dc) % 2,
        )

    partners = (
        [dict(dy=d) for d in (1, 2, 3)]
        + [dict(dc=1)]
        + [dict(dx=d) for d in (1, 2, 3)]
        + [dict(dz=d) for d in range(1, 8)]
    )

    loads = {}
    n_load = [0]

    def load(name, src, dst):
        c = pltpu.make_async_copy(src, dst, load_sem.at[n_load[0]])
        n_load[0] += 1
        c.start()
        loads[name] = c

    for s in range(SEQ_LOCAL):
        load(("x", s), x_hbm.at[s], x_v.at[s])
    w_hbm = (wq_hbm, wk_hbm, wv_hbm)
    for t in (0, 1):
        load(("w", t, 0), w_hbm[t].at[:, pl.ds(0, DEPTH)], w_v.at[t, 0])
    for c in (1, 2):
        for t in (0, 1):
            load(("w", t, c), w_hbm[t].at[:, pl.ds(c * DEPTH, DEPTH)], w_v.at[t, c])
    for c in range(CHUNKS):
        load(("w", 2, c), w_hbm[2].at[:, pl.ds(c * DEPTH, DEPTH)], w_v.at[2, c])

    barrier = pltpu.get_barrier_semaphore()
    for p in partners:
        pl.semaphore_signal(barrier, inc=1, device_id=dev(**p), device_id_type=MESH)

    count = [0]
    started = []

    def send(src, dst, **where):
        i = count[0]
        count[0] += 1
        c = pltpu.make_async_remote_copy(
            src_ref=src, dst_ref=dst, send_sem=ss.at[i], recv_sem=rs.at[i],
            device_id=dev(**where), device_id_type=MESH,
        )
        c.start()
        started.append(c)
        return c

    for s in range(SEQ_LOCAL):
        loads[("x", s)].wait()
        v = x_v[s]
        mean = jnp.mean(v, axis=-1, keepdims=True)
        cen = v - mean
        var = jnp.mean(cen * cen, axis=-1, keepdims=True)
        n_v[pl.ds(s * RES_LOCAL, RES_LOCAL), :] = (cen * lax.rsqrt(var + EPSILON)).astype(BF16)

    def swap(blocks, j):
        return jnp.concatenate([b[:, 64 * j : 64 * j + 64] for b in blocks], axis=1)

    def project(t, c):
        loads[("w", t, c)].wait()
        full = jnp.dot(n_v[...], w_v[t, c], preferred_element_type=F32).astype(BF16)
        blocks = [full[s * RES_LOCAL : (s + 1) * RES_LOCAL] for s in range(SEQ_LOCAL)]
        for j in range(NY):
            send_v[t, c, j] = swap(blocks, j)

    def home(t, c):
        if t == 0:
            return q_v.at[c]
        return (k_v if t == 1 else v_v).at[c, 0]

    def send_y(t, c):
        out = []
        for d in (1, 2, 3):
            out.append(send(send_v.at[t, c, (y + d) % NY], home(t, c).at[y], dy=d))
        return out

    def keep(t, c):
        home(t, c)[y] = send_v[t, c, y]

    def core_swap(t, c):
        b = (k_v if t == 1 else v_v)
        return send(b.at[c, 0], b.at[c, 1], dc=1)

    starts = [sum(w for _, w in GROUPS[:g]) for g in range(len(GROUPS))]

    def scores(c, g):
        kind, w = GROUPS[g]
        q = q_v[c].reshape(ROWS, DEPTH)
        k = k_v[c].reshape(COLS, DEPTH)[starts[g] : starts[g] + w]
        r = lax.dot_general(q, k, (((1,), (1,)), ((), ())), preferred_element_type=F32)
        r = (r * SCALE).astype(BF16)
        s_v = group_refs[g][0]
        if kind == "x":
            s_v[c] = r.reshape(NX, NZ, 16, w)
        else:
            for i in range(NX):
                s_v[c, :, i] = r[i * 128 : (i + 1) * 128].reshape(NZ, 16, w)

    xr, xl, xo = (x + 1) % NX, (x + 3) % NX, (x + 2) % NX
    lo, hi = pl.ds(0, 4), pl.ds(4, 4)

    def wide(v):
        return v.astype(F32)

    class AlongX:
        def __init__(self, c, refs):
            s_v, p_v, self.rx1, self.rxl, self.rxr, self.tmp, self.xs, self.rz = (r.at[c] for r in refs)
            self.s, self.p = s_v, p_v

        def start(self):
            s = self.s
            self.r1 = send(s.at[xo, lo], self.rx1.at[0], dx=1)
            self.l1 = send(s.at[xo, hi], self.rx1.at[1], dx=3)
            self.r2 = send(s.at[xr, hi], self.rxl.at[hi], dx=1)
            self.l2 = send(s.at[xl, lo], self.rxr.at[lo], dx=3)

        def relay(self):
            s = self.s
            self.r1.wait_recv()
            self.tmp[0] = (wide(s[xr, lo]) + wide(self.rx1[0])).astype(BF16)
            self.r3 = send(self.tmp.at[0], self.rxl.at[lo], dx=1)
            self.l1.wait_recv()
            self.tmp[1] = (wide(s[xl, hi]) + wide(self.rx1[1])).astype(BF16)
            self.l3 = send(self.tmp.at[1], self.rxr.at[hi], dx=3)

        def total(self):
            for cp in (self.r2, self.l2, self.r3, self.l3):
                cp.wait_recv()
            self.xs[...] = (wide(self.s[x]) + wide(self.rxl[...]) + wide(self.rxr[...])).astype(BF16)
            self.z = [
                send(self.xs.at[(z + d) % NZ], self.rz.at[d - 1], dz=d) for d in (4, 3, 5, 2, 6, 1, 7)
            ]

        def final(self):
            v = wide(self.s[x, z]) + wide(self.rxl[z]) + wide(self.rxr[z])
            wait_all(self.z)
            for d in range(7):
                v = v + wide(self.rz[d])
            return v

        def put(self, p):
            self.p[x, z] = p
            mine = self.p.at[x, z]
            self.g = [send(mine, mine, dz=d) for d in (4, 3, 5, 2, 6, 1, 7)]

        def gather(self):
            wait_all(self.g)
            b = self.p.at[x]
            self.ra, self.la = send(b, b, dx=1), send(b, b, dx=3)

        def forward(self):
            self.ra.wait_recv()
            b = self.p.at[xl, lo]
            self.rb = send(b, b, dx=1)
            self.la.wait_recv()
            b = self.p.at[xr, hi]
            self.lb = send(b, b, dx=3)

        def done(self):
            wait_all((self.rb, self.lb))

        def rows(self, i):
            return self.p[i].reshape(128, self.p.shape[-1])

    class AlongZ:
        def __init__(self, c, refs):
            s_v, p_v, self.zr, self.zl, self.tz, self.zs, self.rx = (r.at[c] for r in refs)
            self.s, self.p = s_v, p_v

        def start(self):
            o = (z + 4) % NZ
            self.r = send(self.s.at[o, pl.ds(0, 2)], self.zr.at[0, pl.ds(0, 2)], dz=1)
            self.l = send(self.s.at[o, pl.ds(2, 2)], self.zl.at[0, pl.ds(2, 2)], dz=7)

        def ring(self, k):
            s, tz = self.s, self.tz
            dr, dl = (z + 5 - k) % NZ, (z + 3 + k) % NZ
            self.r.wait_recv()
            if k == 2:
                tz[0, 0, pl.ds(0, 2)] = (
                    wide(s[dr, pl.ds(0, 2)]) + wide(self.zr[0, pl.ds(0, 2)])
                ).astype(BF16)
                tz[0, 0, pl.ds(2, 2)] = s[dr, pl.ds(2, 2)]
            else:
                tz[k - 2, 0] = (wide(s[dr]) + wide(self.zr[k - 2])).astype(BF16)
            self.r = send(tz.at[k - 2, 0], self.zr.at[k - 1], dz=1)
            self.l.wait_recv()
            if k == 2:
                tz[0, 1, pl.ds(2, 2)] = (
                    wide(s[dl, pl.ds(2, 2)]) + wide(self.zl[0, pl.ds(2, 2)])
                ).astype(BF16)
                tz[0, 1, pl.ds(0, 2)] = s[dl, pl.ds(0, 2)]
            else:
                tz[k - 2, 1] = (wide(s[dl]) + wide(self.zl[k - 2])).astype(BF16)
            self.l = send(tz.at[k - 2, 1], self.zl.at[k - 1], dz=7)

        def total(self):
            self.r.wait_recv()
            self.l.wait_recv()
            self.zs[...] = wide(self.s[z]) + wide(self.zr[3]) + wide(self.zl[3])
            self.x = [send(self.zs.at[(x + d) % NX], self.rx.at[d - 1], dx=d) for d in (2, 1, 3)]

        def final(self):
            wait_all(self.x)
            return self.zs[x] + self.rx[0] + self.rx[1] + self.rx[2]

        def put(self, p):
            self.p[z, x] = p
            mine = self.p.at[z, x]
            self.g = [send(mine, mine, dx=d) for d in (2, 1, 3)]

        def gather(self, k):
            p = self.p
            if k == 1:
                wait_all(self.g)
                b = p.at[z]
                self.gr, self.gl = send(b, b, dz=1), send(b, b, dz=7)
                return
            zr, zl = (z + k - 1) % NZ, (z + 9 - k) % NZ
            self.gr.wait_recv()
            b = p.at[zl] if k < 4 else p.at[zl, pl.ds(0, 2)]
            self.gr = send(b, b, dz=1)
            self.gl.wait_recv()
            b = p.at[zr] if k < 4 else p.at[zr, pl.ds(2, 2)]
            self.gl = send(b, b, dz=7)

        def done(self):
            wait_all((self.gr, self.gl))

        def rows(self, i):
            return self.p[:, i].reshape(128, self.p.shape[-1])

    parts = [
        [(AlongX if kind == "x" else AlongZ)(c, refs) for (kind, _), refs in zip(GROUPS, group_refs)]
        for c in range(CHUNKS)
    ]
    by_axis = sorted(range(len(GROUPS)), key=lambda g: GROUPS[g][0] == "x")

    def soft(c):
        vals = {g: parts[c][g].final() for g in by_axis}
        peak = None
        for v in vals.values():
            m = jnp.max(v, axis=-1, keepdims=True)
            peak = m if peak is None else jnp.maximum(peak, m)
        total = 0.0
        for g in vals:
            vals[g] = jnp.exp(vals[g] - peak)
            total = total + jnp.sum(vals[g], axis=-1, keepdims=True)
        for g in vals:
            parts[c][g].put((vals[g] / total).astype(BF16))

    def mix(c):
        v = v_v[c].reshape(COLS, DEPTH)

        for i in (0, 2):
            m = None
            for g, (_, w) in enumerate(GROUPS):
                p = jnp.concatenate([parts[c][g].rows(i), parts[c][g].rows(i + 1)], axis=0)
                r = jnp.dot(p, v[starts[g] : starts[g] + w], preferred_element_type=F32)
                m = r if m is None else m + r
            os_v[c, pl.ds(i, 2)] = m.astype(BF16).reshape(2, RES_LOCAL, DEPTH)
        ob_v[c, y] = os_v[c, y]
        return [send(os_v.at[c, (y + d) % NY], ob_v.at[c, y], dy=d) for d in (1, 2, 3)]

    out_copies = []

    def output(c):
        blocks = [ob_v[c, j] for j in range(NY)]
        for s in range(SEQ_LOCAL):
            m_v[c, pl.ds(s * RES_LOCAL, RES_LOCAL), :] = swap(blocks, s)
        cp = pltpu.make_async_copy(
            m_v.at[c], o_ref.at[:, pl.ds(c * DEPTH, DEPTH)], load_sem.at[13 + c]
        )
        cp.start()
        out_copies.append(cp)

    def wait_all(cps):
        for cp in cps:
            cp.wait_recv()

    qk, vs, kc, vc, ms = {}, {}, {}, {}, {}

    def meet():
        pl.semaphore_wait(barrier, len(partners))

    def projections(c, ts):
        def go():
            for t in ts:
                project(t, c)
                keep(t, c)
        return go

    def qk_send(c):
        def go():
            qk[c] = send_y(1, c) + send_y(0, c)
        return go

    def k_swap(c):
        def go():
            wait_all(qk[c][:3])
            kc[c] = core_swap(1, c)
        return go

    def score(c):
        def go():
            wait_all(qk[c][3:])
            kc[c].wait_recv()
            for g in by_axis:
                scores(c, g)
                parts[c][g].start()
        return go

    def do(c, g, what, *args):
        return lambda: getattr(parts[c][g], what)(*args)

    def softmax(c):
        return lambda: soft(c)

    def v_send(c):
        def go():
            vs[c] = send_y(2, c)
        return go

    def v_swap(c):
        def go():
            wait_all(vs[c])
            vc[c] = core_swap(2, c)
        return go

    def mixing(c):
        def go():
            for p in parts[c]:
                p.done()
            vc[c].wait_recv()
            ms[c] = mix(c)
        return go

    def project_out(c):
        def go():
            wait_all(ms[c])
            output(c)
        return go

    schedule = [
        projections(0, (1, 0)), meet, qk_send(0), projections(1, (1, 0)), qk_send(1), projections(2, (1, 0)),
        qk_send(2), k_swap(0), score(0), do(0, 1, "ring", 2), k_swap(1), do(0, 0, "relay"),
        do(0, 1, "ring", 3), score(1), do(0, 1, "ring", 4), do(1, 1, "ring", 2), k_swap(2), do(0, 0, "total"),
        do(1, 0, "relay"), score(2), do(0, 1, "total"), do(1, 1, "ring", 3), projections(2, (2,)),
        do(2, 1, "ring", 2), do(1, 0, "total"), do(1, 1, "ring", 4), do(2, 0, "relay"), do(2, 1, "ring", 3),
        softmax(0), projections(0, (2,)), do(2, 1, "ring", 4), do(2, 0, "total"), do(1, 1, "total"),
        do(0, 1, "gather", 1), v_send(0), softmax(1), do(2, 1, "total"), do(0, 0, "gather"),
        projections(1, (2,)), softmax(2), v_send(1), do(0, 1, "gather", 2), do(1, 1, "gather", 1),
        do(0, 0, "forward"), do(1, 0, "gather"), do(2, 1, "gather", 1), v_send(2), do(0, 1, "gather", 3),
        v_swap(1), do(2, 0, "gather"), v_swap(0), do(1, 1, "gather", 2), do(2, 1, "gather", 2),
        do(0, 1, "gather", 4), do(1, 1, "gather", 3), do(1, 0, "forward"), do(2, 1, "gather", 3), mixing(0),
        do(1, 1, "gather", 4), do(2, 1, "gather", 4), do(2, 0, "forward"), v_swap(2), mixing(1), mixing(2),
        project_out(0), project_out(1), project_out(2),
    ]
    for step in schedule:
        step()
    for cp in out_copies:
        cp.wait()
    for cp in started:
        cp.wait_send()


def group_scratch(kind, w):
    V = pltpu.VMEM
    if kind == "x":
        shapes = [(NX, NZ, 16, w)] * 2 + [(2, 4, 16, w), (NZ, 16, w), (NZ, 16, w), (2, 4, 16, w), (NZ, 16, w), (7, 16, w)]
        return [V((CHUNKS,) + s, BF16) for s in shapes]
    shapes = [(NZ, NX, 16, w)] * 2 + [(4, NX, 16, w)] * 2 + [(3, 2, NX, 16, w)]
    return [V((CHUNKS,) + s, BF16) for s in shapes] + [V((CHUNKS, n, 16, w), F32) for n in (NX, 3)]


def body(alignment_rows, query_matrix, key_matrix, value_matrix, output_matrix):
    any_spec = pl.BlockSpec(memory_space=pl.ANY)
    V = pltpu.VMEM
    rows = SEQ_LOCAL * RES_LOCAL
    block = (NY, RES_LOCAL, DEPTH)
    scratch = [
        V((SEQ_LOCAL, RES_LOCAL, WIDTH), F32),
        V((rows, WIDTH), BF16),
        V((3, CHUNKS, WIDTH, DEPTH), BF16),
        V((3, CHUNKS) + block, BF16),
        V((CHUNKS,) + block, BF16),
        V((CHUNKS, 2) + block, BF16),
        V((CHUNKS, 2) + block, BF16),
        V((CHUNKS,) + block, BF16),
        V((CHUNKS,) + block, BF16),
        V((CHUNKS, rows, DEPTH), BF16),
        pltpu.SemaphoreType.DMA((16,)),
        pltpu.SemaphoreType.DMA((N_SEMS,)),
        pltpu.SemaphoreType.DMA((N_SEMS,)),
    ]
    for kind, w in GROUPS:
        scratch += group_scratch(kind, w)
    mixed = pl.pallas_call(
        kernel,
        out_shape=jax.ShapeDtypeStruct((rows, WIDTH), BF16),
        in_specs=[any_spec] * 4,
        out_specs=any_spec,
        scratch_shapes=scratch,
        compiler_params=pltpu.CompilerParams(
            collective_id=0, has_side_effects=True, vmem_limit_bytes=56 << 20
        ),
        cost_estimate=pl.CostEstimate(
            flops=5_000_000_000, bytes_accessed=6_000_000, transcendentals=60_000
        ),
    )(alignment_rows, query_matrix, key_matrix, value_matrix)
    out = jnp.dot(mixed, output_matrix, preferred_element_type=F32)
    return out.reshape(alignment_rows.shape)


def solution(mesh):
    in_specs = (P("seq", "res", None), P(), P(), P(), P())
    out_specs = P("seq", "res", None)
    return jax.shard_map(body, mesh=mesh, in_specs=in_specs, out_specs=out_specs, check_vma=False)
```

time: 324 us -> 87.9 us (0.27)
  waiting for transfers between devices: 271 us -> 0 us
  Pallas kernels: 0 us -> 84.7 us
  matrix products: 22.8 us -> 3.06 us
  between operations: 13.2 us -> 0.02 us
  other arithmetic: 11.4 us -> 0 us
  local copies, waits for them, and re-layouts: 3.59 us -> 0.01 us
    psum x1 -> x0, waiting for transfers between devices: 182 us -> none  [body(): summed_scores = lax.psum(partial_scores, 'seq') * scale_val]
    all_gather x2 -> x0, waiting for transfers between devices: 89.1 us -> none  [the longest x1 47.6 us: body(): lax.all_gather(keys_own, 'res', axis=1, tiled=True)]
    pallas_call x0 -> x1, Pallas kernels: none -> 84.7 us  [body(): pl.pallas_call(kernel, out_shape=jax.ShapeDtypeStruct((rows, WIDTH), BF16...]
    dot_general x6 -> x1, matrix products: 22.8 us -> 3.06 us  [body(): out = jnp.dot(mixed, output_matrix, preferred_element_type=F32)]
    sub x1 -> x0, other arithmetic: 6.41 us -> none  [body(): expo = jnp.exp(summed_scores - peak_val)]
    reduce_sum x2 -> x0, other arithmetic: 3.36 us -> none  [the longest x1 1.7 us: layer_normalize(): spread = jnp.mean(centred * centred, axis=-1, keepdims=True)]
  transfers between devices with their start and end apart: 3 -> 0, of which waited for: 3 -> 0; matrix products, arithmetic and copies ran while one was open for 4% -> 0% of each run, Pallas kernels for 0% -> 0%
where the time goes in v2:
time: 87.9 us; the launch traced here: 87.7 us
  Pallas kernels  84.7 us (96%)
  matrix products  3.06 us (3%)
    pallas_call x1, Pallas kernels, body(): pl.pallas_call(kernel, out_shape=jax.ShapeDtypeStruct((rows, WIDTH), BF16...  84.7 us
    dot_general x1, matrix products, body(): out = jnp.dot(mixed, output_matrix, preferred_element_type=F32)  3.06 us

profile of v2, /device:TPU:16, one launch (start us, length us, event | category | flops | bytes accessed | tf_op | source)
XLA Modules:
  0.0 87.7 jit_solution(64675366176483120)
XLA Ops:
  0.0 0.0 copy-start
  0.0 84.7 %shard_map.55 = bf16[512,768]{1,0:T(8,128)(2,1)} custom-call(f32[4,128,768]{2,1,0:T(8,128)} %x_hbm.1, bf16[768,768]{1,0:T(8,128)(2,1)} %wq_hbm.1, bf16[768,768]{1,0:T(8,128)(2,1)} %wk_hbm.1, bf16[768,768]{1,0:T(8,128)(2,1)} %wv_hbm.1), custom_call_target="tpu_custom_call" | custom-call | flops 5000000000 | bytes 6000000 | tf_op jit(solution)/shard_map/pallas_call | solution.py:439
  84.7 0.0 copy-done
  84.7 3.1 %fusion = f32[512,768]{1,0:T(8,128)} fusion(bf16[512,768]{1,0:T(8,128)(2,1)} %shard_map.55, bf16[768,768]{1,0:T(8,128)(2,1)S(1)} %copy-done), kind=kOutput, calls=%fused_computation | convolution fusion | flops 603979776 | bytes 3538944 | tf_op jit(solution)/shard_map/dot_general | solution.py:452
Async XLA Ops:
  0.0 84.7 %copy-start = (bf16[768,768]{1,0:T(8,128)(2,1)S(1)}, bf16[768,768]{1,0:T(8,128)(2,1)}, u32[]{:S(2)}) copy-start(bf16[768,768]{1,0:T(8,128)(2,1)} %param.9) | copy-start | bytes 3538948

commit v3 on v2

--- a/solution.py
+++ b/solution.py
@@ -19,25 +19,38 @@
 DEPTH = 256
 SCALE = 1.0 / math.sqrt(64 * 128)
 EPSILON = 1e-05
-N_SEMS = 216
-
-GROUPS = (("x", 768), ("z", 256),)
+N_SEMS = 242
+
+SUMS = (
+    (("x", 640), ("z", 384),),
+    (("x", 640), ("z", 384),),
+    (("x", 640), ("z", 384),),
+)
+SPREADS = (
+    (("x", 640), ("z", 384),),
+    (("x", 640), ("z", 384),),
+    (("x", 640), ("z", 384),),
+)
 
 
 def kernel(x_hbm, wq_hbm, wk_hbm, wv_hbm, o_ref, *scratch):
     (x_v, n_v, w_v, send_v, q_v, k_v, v_v, os_v, ob_v, m_v, load_sem, ss, rs) = scratch[:13]
-    group_refs, at = [], 13
-    for kind, _ in GROUPS:
-        size = 8 if kind == "x" else 7
-        group_refs.append(scratch[at : at + size])
-        at += size
+    at = 13
+    sum_refs, spread_refs = [], []
+    for table, store, sizes in ((SUMS, sum_refs, {"x": 7, "z": 6}), (SPREADS, spread_refs, {"x": 1, "z": 1})):
+        for row in table:
+            store.append([])
+            for kind, _ in row:
+                store[-1].append(scratch[at : at + sizes[kind]])
+                at += sizes[kind]
     s_id, r_id = lax.axis_index("seq"), lax.axis_index("res")
-    z, x = s_id // NX, s_id % NX
+    z, chip_x = s_id // NX, s_id % NX
     y, core = r_id // 2, r_id % 2
+    x = (chip_x + y) % NX
 
     def dev(dz=0, dx=0, dy=0, dc=0):
         return (
-            ((z + dz) % NZ) * NX + (x + dx) % NX,
+            ((z + dz) % NZ) * NX + (chip_x + dx) % NX,
             ((y + dy) % NY) * 2 + (core + dc) % 2,
         )
 
@@ -122,20 +135,28 @@
         b = (k_v if t == 1 else v_v)
         return send(b.at[c, 0], b.at[c, 1], dc=1)
 
-    starts = [sum(w for _, w in GROUPS[:g]) for g in range(len(GROUPS))]
+    def starts(row):
+        return [sum(w for _, w in row[:g]) for g in range(len(row))]
 
     def scores(c, g):
-        kind, w = GROUPS[g]
+        kind, w = SUMS[c][g]
+        first = starts(SUMS[c])[g]
         q = q_v[c].reshape(ROWS, DEPTH)
-        k = k_v[c].reshape(COLS, DEPTH)[starts[g] : starts[g] + w]
+        k = k_v[c].reshape(COLS, DEPTH)[first : first + w]
         r = lax.dot_general(q, k, (((1,), (1,)), ((), ())), preferred_element_type=F32)
         r = (r * SCALE).astype(BF16)
-        s_v = group_refs[g][0]
+        s_v = sum_refs[c][g][0]
         if kind == "x":
-            s_v[c] = r.reshape(NX, NZ, 16, w)
+            s_v[...] = r.reshape(NX, NZ, 16, w)
         else:
             for i in range(NX):
-                s_v[c, :, i] = r[i * 128 : (i + 1) * 128].reshape(NZ, 16, w)
+                s_v[:, i] = r[i * 128 : (i + 1) * 128].reshape(NZ, 16, w)
+
+    every = pl.ds(0, 16)
+
+    def halves(w):
+        first = w // 256 * 128
+        return pl.ds(0, first), pl.ds(first, w - first)
 
     xr, xl, xo = (x + 1) % NX, (x + 3) % NX, (x + 2) % NX
     lo, hi = pl.ds(0, 4), pl.ds(4, 4)
@@ -143,10 +164,10 @@
     def wide(v):
         return v.astype(F32)
 
-    class AlongX:
-        def __init__(self, c, refs):
-            s_v, p_v, self.rx1, self.rxl, self.rxr, self.tmp, self.xs, self.rz = (r.at[c] for r in refs)
-            self.s, self.p = s_v, p_v
+    class SumX:
+        def __init__(self, refs):
+            self.s, self.rx1, self.rxl, self.rxr, self.tmp, self.xs, self.zz = refs
+            self.half = halves(self.s.shape[-1])
 
         def start(self):
             s = self.s
@@ -168,45 +189,40 @@
             for cp in (self.r2, self.l2, self.r3, self.l3):
                 cp.wait_recv()
             self.xs[...] = (wide(self.s[x]) + wide(self.rxl[...]) + wide(self.rxr[...])).astype(BF16)
-            self.z = [
-                send(self.xs.at[(z + d) % NZ], self.rz.at[d - 1], dz=d) for d in (4, 3, 5, 2, 6, 1, 7)
-            ]
+            xs, zz, (a, b) = self.xs, self.zz, self.half
+            far = xs.at[(z + 4) % NZ]
+            self.h = (send(far.at[every, a], zz.at[0, every, a], dz=2), send(far.at[every, b], zz.at[1, every, b], dz=6))
+            self.t = (
+                send(xs.at[(z + 3) % NZ], zz.at[2], dz=1),
+                send(xs.at[(z + 5) % NZ], zz.at[3], dz=7),
+            )
+            self.d = (
+                send(xs.at[(z + 1) % NZ], zz.at[4], dz=1),
+                send(xs.at[(z + 7) % NZ], zz.at[5], dz=7),
+            )
+
+        def relay_z(self):
+            zz = self.zz
+            self.f = []
+            for i in (0, 1):
+                block = self.xs.at[(z + 2 + 4 * i) % NZ]
+                wait_all((self.h[i], self.t[i]))
+                near, far = self.half[1 - i], self.half[i]
+                zz[6 + i, :, far] = (wide(block[:, far]) + wide(zz[2 + i, :, far]) + wide(zz[i, :, far])).astype(BF16)
+                zz[6 + i, :, near] = (wide(block[:, near]) + wide(zz[2 + i, :, near])).astype(BF16)
+                self.f.append(send(zz.at[6 + i], zz.at[8 + i], dz=2 + 4 * i))
 
         def final(self):
             v = wide(self.s[x, z]) + wide(self.rxl[z]) + wide(self.rxr[z])
-            wait_all(self.z)
-            for d in range(7):
-                v = v + wide(self.rz[d])
+            wait_all(self.d)
+            wait_all(self.f)
+            for k in (4, 5, 8, 9):
+                v = v + wide(self.zz[k])
             return v
 
-        def put(self, p):
-            self.p[x, z] = p
-            mine = self.p.at[x, z]
-            self.g = [send(mine, mine, dz=d) for d in (4, 3, 5, 2, 6, 1, 7)]
-
-        def gather(self):
-            wait_all(self.g)
-            b = self.p.at[x]
-            self.ra, self.la = send(b, b, dx=1), send(b, b, dx=3)
-
-        def forward(self):
-            self.ra.wait_recv()
-            b = self.p.at[xl, lo]
-            self.rb = send(b, b, dx=1)
-            self.la.wait_recv()
-            b = self.p.at[xr, hi]
-            self.lb = send(b, b, dx=3)
-
-        def done(self):
-            wait_all((self.rb, self.lb))
-
-        def rows(self, i):
-            return self.p[i].reshape(128, self.p.shape[-1])
-
-    class AlongZ:
-        def __init__(self, c, refs):
-            s_v, p_v, self.zr, self.zl, self.tz, self.zs, self.rx = (r.at[c] for r in refs)
-            self.s, self.p = s_v, p_v
+    class SumZ:
+        def __init__(self, refs):
+            self.s, self.zr, self.zl, self.tz, self.zs, self.rx = refs
 
         def start(self):
             o = (z + 4) % NZ
@@ -245,6 +261,51 @@
             wait_all(self.x)
             return self.zs[x] + self.rx[0] + self.rx[1] + self.rx[2]
 
+    class SpreadX:
+        def __init__(self, refs):
+            (self.p,) = refs
+            self.half = halves(self.p.shape[-1])
+
+        def put(self, p):
+            self.p[x, z] = p
+            mine = self.p.at[x, z]
+            self.two = (send(mine, mine, dz=2), send(mine, mine, dz=6))
+            self.g = [send(mine, mine, dz=1), send(mine, mine, dz=7)]
+
+        def pass_on(self):
+            for i in (0, 1):
+                self.two[i].wait_recv()
+                block = self.p.at[x, (z + 6 - 4 * i) % NZ]
+                half = block.at[every, self.half[i]]
+                self.g.append(send(half, half, dz=2 + 4 * i))
+                self.g.append(send(block, block, dz=1 + 6 * i))
+
+        def gather(self):
+            wait_all(self.g)
+            b = self.p.at[x]
+            self.ra, self.la = send(b, b, dx=1), send(b, b, dx=3)
+
+        def forward(self):
+            self.ra.wait_recv()
+            b = self.p.at[xl, lo]
+            self.rb = send(b, b, dx=1)
+            self.la.wait_recv()
+            b = self.p.at[xr, hi]
+            self.lb = send(b, b, dx=3)
+
+        def near(self):
+            pass
+
+        def done(self):
+            wait_all((self.rb, self.lb))
+
+        def rows(self, i):
+            return self.p[i].reshape(128, self.p.shape[-1])
+
+    class SpreadZ:
+        def __init__(self, refs):
+            (self.p,) = refs
+
         def put(self, p):
             self.p[z, x] = p
             mine = self.p.at[z, x]
@@ -265,43 +326,77 @@
             b = p.at[zr] if k < 4 else p.at[zr, pl.ds(2, 2)]
             self.gl = send(b, b, dz=7)
 
+        def near(self):
+            wait_all((self.gr, self.gl))
+
         def done(self):
-            wait_all((self.gr, self.gl))
+            pass
 
         def rows(self, i):
             return self.p[:, i].reshape(128, self.p.shape[-1])
 
-    parts = [
-        [(AlongX if kind == "x" else AlongZ)(c, refs) for (kind, _), refs in zip(GROUPS, group_refs)]
+    sums = [
+        [(SumX if kind == "x" else SumZ)(refs) for (kind, _), refs in zip(SUMS[c], sum_refs[c])]
         for c in range(CHUNKS)
     ]
-    by_axis = sorted(range(len(GROUPS)), key=lambda g: GROUPS[g][0] == "x")
+    spreads = [
+        [
+            (SpreadX if kind == "x" else SpreadZ)(refs)
+            for (kind, _), refs in zip(SPREADS[c], spread_refs[c])
+        ]
+        for c in range(CHUNKS)
+    ]
+
+    def z_first(c):
+        return sorted(range(len(SUMS[c])), key=lambda g: SUMS[c][g][0] == "x")
 
     def soft(c):
-        vals = {g: parts[c][g].final() for g in by_axis}
-        peak = None
-        for v in vals.values():
-            m = jnp.max(v, axis=-1, keepdims=True)
-            peak = m if peak is None else jnp.maximum(peak, m)
-        total = 0.0
-        for g in vals:
-            vals[g] = jnp.exp(vals[g] - peak)
-            total = total + jnp.sum(vals[g], axis=-1, keepdims=True)
-        for g in vals:
-            parts[c][g].put((vals[g] / total).astype(BF16))
-
-    def mix(c):
+        vals = {g: sums[c][g].final() for g in z_first(c)}
+        v = jnp.concatenate([vals[g] for g in range(len(vals))], axis=1)
+        e = jnp.exp(v - jnp.max(v, axis=-1, keepdims=True))
+        p = (e / jnp.sum(e, axis=-1, keepdims=True)).astype(BF16)
+        for g, (_, w) in enumerate(SPREADS[c]):
+            first = starts(SPREADS[c])[g]
+            spreads[c][g].put(p[:, first : first + w])
+
+    back = {}
+
+    def mix_rows(c, i):
         v = v_v[c].reshape(COLS, DEPTH)
-
-        for i in (0, 2):
-            m = None
-            for g, (_, w) in enumerate(GROUPS):
-                p = jnp.concatenate([parts[c][g].rows(i), parts[c][g].rows(i + 1)], axis=0)
-                r = jnp.dot(p, v[starts[g] : starts[g] + w], preferred_element_type=F32)
-                m = r if m is None else m + r
-            os_v[c, pl.ds(i, 2)] = m.astype(BF16).reshape(2, RES_LOCAL, DEPTH)
-        ob_v[c, y] = os_v[c, y]
-        return [send(os_v.at[c, (y + d) % NY], ob_v.at[c, y], dy=d) for d in (1, 2, 3)]
+        m = None
+        for g, (_, w) in enumerate(SPREADS[c]):
+            first = starts(SPREADS[c])[g]
+            r = jnp.dot(spreads[c][g].rows(i), v[first : first + w], preferred_element_type=F32)
+            m = r if m is None else m + r
+        os_v[c, i] = m.astype(BF16)
+        d = (i - y + NY) % NY
+        base = back[c]
+
+        @pl.when(d == 0)
+        def _():
+            ob_v[c, y] = os_v[c, i]
+
+        @pl.when(d != 0)
+        def _():
+            s_, r_ = dev()
+            pltpu.make_async_remote_copy(
+                src_ref=os_v.at[c, i], dst_ref=ob_v.at[c, y],
+                send_sem=ss.at[base + d - 1], recv_sem=rs.at[base + d - 1],
+                device_id=(s_, i * 2 + core), device_id_type=MESH,
+            ).start()
+
+    def mix_start(c):
+        back[c] = count[0]
+        count[0] += 3
+        ms[c] = [
+            pltpu.make_async_remote_copy(
+                src_ref=os_v.at[c, (y + d) % NY], dst_ref=ob_v.at[c, y],
+                send_sem=ss.at[back[c] + d - 1], recv_sem=rs.at[back[c] + d - 1],
+                device_id=dev(dy=d), device_id_type=MESH,
+            )
+            for d in (1, 2, 3)
+        ]
+        started.extend(ms[c])
 
     out_copies = []
 
@@ -346,13 +441,16 @@
         def go():
             wait_all(qk[c][3:])
             kc[c].wait_recv()
-            for g in by_axis:
+            for g in z_first(c):
                 scores(c, g)
-                parts[c][g].start()
-        return go
-
-    def do(c, g, what, *args):
-        return lambda: getattr(parts[c][g], what)(*args)
+                sums[c][g].start()
+        return go
+
+    def add(c, g, what, *args):
+        return lambda: getattr(sums[c][g], what)(*args)
+
+    def spread(c, g, what, *args):
+        return lambda: getattr(spreads[c][g], what)(*args)
 
     def softmax(c):
         return lambda: soft(c)
@@ -368,12 +466,26 @@
             vc[c] = core_swap(2, c)
         return go
 
-    def mixing(c):
-        def go():
-            for p in parts[c]:
+    def mix_own(c):
+        def go():
+            for p in spreads[c]:
+                p.near()
+            vc[c].wait_recv()
+            mix_start(c)
+            mix_rows(c, x)
+        return go
+
+    def mix_near(c):
+        def go():
+            mix_rows(c, xl)
+            mix_rows(c, xr)
+        return go
+
+    def mix_far(c):
+        def go():
+            for p in spreads[c]:
                 p.done()
-            vc[c].wait_recv()
-            ms[c] = mix(c)
+            mix_rows(c, xo)
         return go
 
     def project_out(c):
@@ -383,19 +495,22 @@
         return go
 
     schedule = [
-        projections(0, (1, 0)), meet, qk_send(0), projections(1, (1, 0)), qk_send(1), projections(2, (1, 0)),
-        qk_send(2), k_swap(0), score(0), do(0, 1, "ring", 2), k_swap(1), do(0, 0, "relay"),
-        do(0, 1, "ring", 3), score(1), do(0, 1, "ring", 4), do(1, 1, "ring", 2), k_swap(2), do(0, 0, "total"),
-        do(1, 0, "relay"), score(2), do(0, 1, "total"), do(1, 1, "ring", 3), projections(2, (2,)),
-        do(2, 1, "ring", 2), do(1, 0, "total"), do(1, 1, "ring", 4), do(2, 0, "relay"), do(2, 1, "ring", 3),
-        softmax(0), projections(0, (2,)), do(2, 1, "ring", 4), do(2, 0, "total"), do(1, 1, "total"),
-        do(0, 1, "gather", 1), v_send(0), softmax(1), do(2, 1, "total"), do(0, 0, "gather"),
-        projections(1, (2,)), softmax(2), v_send(1), do(0, 1, "gather", 2), do(1, 1, "gather", 1),
-        do(0, 0, "forward"), do(1, 0, "gather"), do(2, 1, "gather", 1), v_send(2), do(0, 1, "gather", 3),
-        v_swap(1), do(2, 0, "gather"), v_swap(0), do(1, 1, "gather", 2), do(2, 1, "gather", 2),
-        do(0, 1, "gather", 4), do(1, 1, "gather", 3), do(1, 0, "forward"), do(2, 1, "gather", 3), mixing(0),
-        do(1, 1, "gather", 4), do(2, 1, "gather", 4), do(2, 0, "forward"), v_swap(2), mixing(1), mixing(2),
-        project_out(0), project_out(1), project_out(2),
+        projections(0, (1, 0)), meet, qk_send(0), projections(1, (1, 0)), projections(2, (1, 0)), qk_send(1),
+        k_swap(0), score(0), qk_send(2), k_swap(1), add(0, 1, "ring", 2), projections(2, (2,)),
+        add(0, 0, "relay"), score(1), projections(1, (2,)), add(0, 1, "ring", 3), k_swap(2),
+        projections(0, (2,)), add(1, 1, "ring", 2), add(0, 0, "total"), add(1, 0, "relay"), score(2),
+        add(0, 1, "ring", 4), add(1, 1, "ring", 3), v_send(0), v_send(1), add(0, 0, "relay_z"),
+        add(2, 1, "ring", 2), add(1, 0, "total"), add(0, 1, "total"), add(2, 0, "relay"), add(1, 1, "ring", 4),
+        add(2, 1, "ring", 3), add(1, 0, "relay_z"), softmax(0), add(1, 1, "total"), add(2, 0, "total"),
+        add(2, 1, "ring", 4), spread(0, 1, "gather", 1), spread(0, 0, "pass_on"), v_send(2),
+        add(2, 0, "relay_z"), v_swap(0), softmax(1), add(2, 1, "total"), spread(0, 1, "gather", 2),
+        spread(0, 0, "gather"), spread(1, 1, "gather", 1), spread(1, 0, "pass_on"), softmax(2), v_swap(2),
+        spread(0, 1, "gather", 3), spread(1, 1, "gather", 2), v_swap(1), spread(1, 0, "gather"),
+        spread(2, 1, "gather", 1), spread(2, 0, "pass_on"), spread(0, 1, "gather", 4),
+        spread(1, 1, "gather", 3), spread(2, 1, "gather", 2), spread(0, 0, "forward"), spread(2, 0, "gather"),
+        mix_own(0), mix_near(0), spread(1, 1, "gather", 4), spread(1, 0, "forward"), spread(2, 1, "gather", 3),
+        mix_far(0), mix_own(1), mix_near(1), spread(2, 1, "gather", 4), spread(2, 0, "forward"), mix_far(1),
+        mix_own(2), mix_near(2), project_out(0), mix_far(2), project_out(1), project_out(2),
     ]
     for step in schedule:
         step()
@@ -405,13 +520,17 @@
         cp.wait_send()
 
 
-def group_scratch(kind, w):
+def sum_scratch(kind, w):
     V = pltpu.VMEM
     if kind == "x":
-        shapes = [(NX, NZ, 16, w)] * 2 + [(2, 4, 16, w), (NZ, 16, w), (NZ, 16, w), (2, 4, 16, w), (NZ, 16, w), (7, 16, w)]
-        return [V((CHUNKS,) + s, BF16) for s in shapes]
-    shapes = [(NZ, NX, 16, w)] * 2 + [(4, NX, 16, w)] * 2 + [(3, 2, NX, 16, w)]
-    return [V((CHUNKS,) + s, BF16) for s in shapes] + [V((CHUNKS, n, 16, w), F32) for n in (NX, 3)]
+        shapes = [(NX, NZ, 16, w), (2, 4, 16, w), (NZ, 16, w), (NZ, 16, w), (2, 4, 16, w), (NZ, 16, w), (10, 16, w)]
+        return [V(s, BF16) for s in shapes]
+    shapes = [(NZ, NX, 16, w), (4, NX, 16, w), (4, NX, 16, w), (3, 2, NX, 16, w)]
+    return [V(s, BF16) for s in shapes] + [V((n, 16, w), F32) for n in (NX, 3)]
+
+
+def spread_scratch(kind, w):
+    return [pltpu.VMEM((NZ, NX, 16, w) if kind == "z" else (NX, NZ, 16, w), BF16)]
 
 
 def body(alignment_rows, query_matrix, key_matrix, value_matrix, output_matrix):
@@ -434,8 +553,10 @@
         pltpu.SemaphoreType.DMA((N_SEMS,)),
         pltpu.SemaphoreType.DMA((N_SEMS,)),
     ]
-    for kind, w in GROUPS:
-        scratch += group_scratch(kind, w)
+    for table, make in ((SUMS, sum_scratch), (SPREADS, spread_scratch)):
+        for row in table:
+            for kind, w in row:
+                scratch += make(kind, w)
     mixed = pl.pallas_call(
         kernel,
         out_shape=jax.ShapeDtypeStruct((rows, WIDTH), BF16),

time: 87.9 us -> 82.3 us (0.936)
  Pallas kernels: 84.7 us -> 78.8 us
    pallas_call x1, Pallas kernels: 84.7 us -> 78.8 us  [body(): pl.pallas_call(kernel, out_shape=jax.ShapeDtypeStruct((rows, WIDTH), BF16...]
where the time goes in v3:
time: 82.3 us; the launch traced here: 81.9 us
  Pallas kernels  78.8 us (96%)
  matrix products  3.06 us (4%)
    pallas_call x1, Pallas kernels, body(): pl.pallas_call(kernel, out_shape=jax.ShapeDtypeStruct((rows, WIDTH), BF16...  78.8 us
    dot_general x1, matrix products, body(): out = jnp.dot(mixed, output_matrix, preferred_element_type=F32)  3.06 us

profile of v3, /device:TPU:16, one launch (start us, length us, event | category | flops | bytes accessed | tf_op | source)
XLA Modules:
  0.0 81.9 jit_solution(10532854358046146304)
XLA Ops:
  0.0 0.0 copy-start
  0.0 78.8 %shard_map.55 = bf16[512,768]{1,0:T(8,128)(2,1)} custom-call(f32[4,128,768]{2,1,0:T(8,128)} %x_hbm.1, bf16[768,768]{1,0:T(8,128)(2,1)} %wq_hbm.1, bf16[768,768]{1,0:T(8,128)(2,1)} %wk_hbm.1, bf16[768,768]{1,0:T(8,128)(2,1)} %wv_hbm.1), custom_call_target="tpu_custom_call" | custom-call | flops 5000000000 | bytes 6000000 | tf_op jit(solution)/shard_map/pallas_call | solution.py:560
  78.9 0.0 copy-done
  78.9 3.1 %fusion = f32[512,768]{1,0:T(8,128)} fusion(bf16[512,768]{1,0:T(8,128)(2,1)} %shard_map.55, bf16[768,768]{1,0:T(8,128)(2,1)S(1)} %copy-done), kind=kOutput, calls=%fused_computation | convolution fusion | flops 603979776 | bytes 3538944 | tf_op jit(solution)/shard_map/dot_general | solution.py:573
Async XLA Ops:
  0.0 78.9 %copy-start = (bf16[768,768]{1,0:T(8,128)(2,1)S(1)}, bf16[768,768]{1,0:T(8,128)(2,1)}, u32[]{:S(2)}) copy-start(bf16[768,768]{1,0:T(8,128)(2,1)} %param.9) | copy-start | bytes 3538948

commit v4 on v3

--- a/solution.py
+++ b/solution.py
@@ -27,9 +27,9 @@
     (("x", 640), ("z", 384),),
 )
 SPREADS = (
+    (("x", 768), ("z", 256),),
     (("x", 640), ("z", 384),),
-    (("x", 640), ("z", 384),),
-    (("x", 640), ("z", 384),),
+    (("x", 768), ("z", 256),),
 )
 
 
@@ -419,6 +419,15 @@
     def meet():
         pl.semaphore_wait(barrier, len(partners))
 
+    def first():
+        project(1, 0)
+        meet()
+        qk[0] = send_y(1, 0)
+        project(0, 0)
+        qk[0] += send_y(0, 0)
+        keep(1, 0)
+        keep(0, 0)
+
     def projections(c, ts):
         def go():
             for t in ts:
@@ -495,22 +504,22 @@
         return go
 
     schedule = [
-        projections(0, (1, 0)), meet, qk_send(0), projections(1, (1, 0)), projections(2, (1, 0)), qk_send(1),
-        k_swap(0), score(0), qk_send(2), k_swap(1), add(0, 1, "ring", 2), projections(2, (2,)),
-        add(0, 0, "relay"), score(1), projections(1, (2,)), add(0, 1, "ring", 3), k_swap(2),
-        projections(0, (2,)), add(1, 1, "ring", 2), add(0, 0, "total"), add(1, 0, "relay"), score(2),
-        add(0, 1, "ring", 4), add(1, 1, "ring", 3), v_send(0), v_send(1), add(0, 0, "relay_z"),
-        add(2, 1, "ring", 2), add(1, 0, "total"), add(0, 1, "total"), add(2, 0, "relay"), add(1, 1, "ring", 4),
-        add(2, 1, "ring", 3), add(1, 0, "relay_z"), softmax(0), add(1, 1, "total"), add(2, 0, "total"),
-        add(2, 1, "ring", 4), spread(0, 1, "gather", 1), spread(0, 0, "pass_on"), v_send(2),
-        add(2, 0, "relay_z"), v_swap(0), softmax(1), add(2, 1, "total"), spread(0, 1, "gather", 2),
-        spread(0, 0, "gather"), spread(1, 1, "gather", 1), spread(1, 0, "pass_on"), softmax(2), v_swap(2),
-        spread(0, 1, "gather", 3), spread(1, 1, "gather", 2), v_swap(1), spread(1, 0, "gather"),
-        spread(2, 1, "gather", 1), spread(2, 0, "pass_on"), spread(0, 1, "gather", 4),
-        spread(1, 1, "gather", 3), spread(2, 1, "gather", 2), spread(0, 0, "forward"), spread(2, 0, "gather"),
-        mix_own(0), mix_near(0), spread(1, 1, "gather", 4), spread(1, 0, "forward"), spread(2, 1, "gather", 3),
-        mix_far(0), mix_own(1), mix_near(1), spread(2, 1, "gather", 4), spread(2, 0, "forward"), mix_far(1),
-        mix_own(2), mix_near(2), project_out(0), mix_far(2), project_out(1), project_out(2),
+        first, projections(1, (1, 0)), qk_send(1), projections(2, (1, 0)), qk_send(2), projections(0, (2,)),
+        k_swap(0), score(0), k_swap(1), add(0, 1, "ring", 2), add(0, 0, "relay"), score(1),
+        add(0, 1, "ring", 3), projections(1, (2,)), k_swap(2), add(1, 1, "ring", 2), add(0, 0, "total"),
+        v_send(0), add(1, 0, "relay"), score(2), add(0, 1, "ring", 4), add(1, 1, "ring", 3),
+        add(0, 0, "relay_z"), add(2, 1, "ring", 2), add(1, 0, "total"), v_swap(0), add(0, 1, "total"),
+        add(1, 1, "ring", 4), add(2, 0, "relay"), add(2, 1, "ring", 3), add(1, 0, "relay_z"), softmax(0),
+        add(1, 1, "total"), add(2, 0, "total"), add(2, 1, "ring", 4), spread(0, 0, "pass_on"),
+        projections(2, (2,)), spread(0, 1, "gather", 1), softmax(1), add(2, 1, "total"), add(2, 0, "relay_z"),
+        spread(0, 0, "gather"), spread(0, 1, "gather", 2), spread(1, 1, "gather", 1), spread(1, 0, "pass_on"),
+        v_send(1), softmax(2), spread(1, 1, "gather", 2), v_send(2), spread(0, 1, "gather", 3),
+        spread(1, 0, "gather"), spread(0, 0, "forward"), spread(2, 1, "gather", 1), spread(2, 0, "pass_on"),
+        spread(1, 1, "gather", 3), spread(0, 1, "gather", 4), spread(2, 1, "gather", 2),
+        spread(2, 0, "gather"), v_swap(1), mix_own(0), spread(1, 1, "gather", 4), spread(2, 1, "gather", 3),
+        mix_near(0), spread(1, 0, "forward"), v_swap(2), spread(2, 1, "gather", 4), mix_own(1), mix_far(0),
+        spread(2, 0, "forward"), mix_near(1), mix_far(1), mix_own(2), mix_near(2), mix_far(2), project_out(1),
+        project_out(0), project_out(2),
     ]
     for step in schedule:
         step()
@@ -535,6 +544,7 @@
 
 def body(alignment_rows, query_matrix, key_matrix, value_matrix, output_matrix):
     any_spec = pl.BlockSpec(memory_space=pl.ANY)
+    hbm_spec = pl.BlockSpec(memory_space=pltpu.HBM)
     V = pltpu.VMEM
     rows = SEQ_LOCAL * RES_LOCAL
     block = (NY, RES_LOCAL, DEPTH)
@@ -557,19 +567,23 @@
         for row in table:
             for kind, w in row:
                 scratch += make(kind, w)
+    inputs = [
+        pltpu.with_memory_space_constraint(a, pltpu.HBM)
+        for a in (alignment_rows, query_matrix, key_matrix, value_matrix)
+    ]
     mixed = pl.pallas_call(
         kernel,
         out_shape=jax.ShapeDtypeStruct((rows, WIDTH), BF16),
-        in_specs=[any_spec] * 4,
+        in_specs=[hbm_spec] * 4,
         out_specs=any_spec,
         scratch_shapes=scratch,
         compiler_params=pltpu.CompilerParams(
-            collective_id=0, has_side_effects=True, vmem_limit_bytes=56 << 20
+            collective_id=0, has_side_effects=True, vmem_limit_bytes=34 << 20
         ),
         cost_estimate=pl.CostEstimate(
             flops=5_000_000_000, bytes_accessed=6_000_000, transcendentals=60_000
         ),
-    )(alignment_rows, query_matrix, key_matrix, value_matrix)
+    )(*inputs)
     out = jnp.dot(mixed, output_matrix, preferred_element_type=F32)
     return out.reshape(alignment_rows.shape)
 

time: 82.3 us -> 79.4 us (0.965)
  Pallas kernels: 78.8 us -> 77.3 us
  matrix products: 3.06 us -> 1.92 us
    pallas_call x1, Pallas kernels: 78.8 us -> 77.3 us  [body(): pl.pallas_call(kernel, out_shape=jax.ShapeDtypeStruct((rows, WIDTH), BF16...]
    dot_general x1, matrix products: 3.06 us -> 1.92 us  [body(): out = jnp.dot(mixed, output_matrix, preferred_element_type=F32)]
where the time goes in v4:
time: 79.4 us; the launch traced here: 79.3 us
  Pallas kernels  77.3 us (97%)
  matrix products  1.92 us (2%)
    pallas_call x1, Pallas kernels, body(): pl.pallas_call(kernel, out_shape=jax.ShapeDtypeStruct((rows, WIDTH), BF16...  77.3 us
    dot_general x1, matrix products, body(): out = jnp.dot(mixed, output_matrix, preferred_element_type=F32)  1.92 us

profile of v4, /device:TPU:16, one launch (start us, length us, event | category | flops | bytes accessed | tf_op | source)
XLA Modules:
  0.0 79.3 jit_solution(3493369626071628875)
XLA Ops:
  0.0 0.0 copy-start
  0.0 77.3 %shard_map.55 = bf16[512,768]{1,0:T(8,128)(2,1)S(1)} custom-call(f32[4,128,768]{2,1,0:T(8,128)} %x_hbm.1, bf16[768,768]{1,0:T(8,128)(2,1)} %wq_hbm.1, bf16[768,768]{1,0:T(8,128)(2,1)} %wk_hbm.1, bf16[768,768]{1,0:T(8,128)(2,1)} %wv_hbm.1), custom_call_target="tpu_custom_call" | custom-call | flops 5000000000 | bytes 6000000 | tf_op jit(solution)/shard_map/pallas_call | solution.py:574
  77.4 0.0 copy-done
  77.4 1.9 %fusion = f32[512,768]{1,0:T(8,128)} fusion(bf16[512,768]{1,0:T(8,128)(2,1)S(1)} %shard_map.55, bf16[768,768]{1,0:T(8,128)(2,1)S(1)} %copy-done), kind=kOutput, calls=%fused_computation | convolution fusion | flops 603979776 | bytes 3538944 | tf_op jit(solution)/shard_map/dot_general | solution.py:587
Async XLA Ops:
  0.0 77.4 %copy-start = (bf16[768,768]{1,0:T(8,128)(2,1)S(1)}, bf16[768,768]{1,0:T(8,128)(2,1)}, u32[]{:S(2)}) copy-start(bf16[768,768]{1,0:T(8,128)(2,1)} %param.9) | copy-start | bytes 3538948

commit v5 on v4

--- a/solution.py
+++ b/solution.py
@@ -19,23 +19,22 @@
 DEPTH = 256
 SCALE = 1.0 / math.sqrt(64 * 128)
 EPSILON = 1e-05
-N_SEMS = 242
+N_SEMS = 194
 
 SUMS = (
-    (("x", 640), ("z", 384),),
-    (("x", 640), ("z", 384),),
+    (("x", 512), ("z", 512),),
+    (("x", 512), ("z", 512),),
+)
+SPREADS = (
+    (("x", 512), ("z", 512),),
     (("x", 640), ("z", 384),),
 )
-SPREADS = (
-    (("x", 768), ("z", 256),),
-    (("x", 640), ("z", 384),),
-    (("x", 768), ("z", 256),),
-)
 
 
 def kernel(x_hbm, wq_hbm, wk_hbm, wv_hbm, o_ref, *scratch):
     (x_v, n_v, w_v, send_v, q_v, k_v, v_v, os_v, ob_v, m_v, load_sem, ss, rs) = scratch[:13]
-    at = 13
+    q2, k2, v2, s2, zz2, p2 = scratch[13:19]
+    at = 19
     sum_refs, spread_refs = [], []
     for table, store, sizes in ((SUMS, sum_refs, {"x": 7, "z": 6}), (SPREADS, spread_refs, {"x": 1, "z": 1})):
         for row in table:
@@ -58,7 +57,7 @@
         [dict(dy=d) for d in (1, 2, 3)]
         + [dict(dc=1)]
         + [dict(dx=d) for d in (1, 2, 3)]
-        + [dict(dz=d) for d in range(1, 8)]
+        + [dict(dz=d) for d in (1, 2, 6, 7)]
     )
 
     loads = {}
@@ -128,8 +127,17 @@
             out.append(send(send_v.at[t, c, (y + d) % NY], home(t, c).at[y], dy=d))
         return out
 
+    def last_home(t):
+        return (q2.at[chip_x], k2.at[0, chip_x, y], v2.at[0, chip_x, y])[t]
+
+    def send_x(t):
+        return [send(send_v.at[t, 2, (chip_x + d) % NX], last_home(t), dx=d) for d in (1, 2, 3)]
+
     def keep(t, c):
-        home(t, c)[y] = send_v[t, c, y]
+        if c == 2:
+            last_home(t)[...] = send_v[t, 2, chip_x]
+        else:
+            home(t, c)[y] = send_v[t, c, y]
 
     def core_swap(t, c):
         b = (k_v if t == 1 else v_v)
@@ -189,6 +197,9 @@
             for cp in (self.r2, self.l2, self.r3, self.l3):
                 cp.wait_recv()
             self.xs[...] = (wide(self.s[x]) + wide(self.rxl[...]) + wide(self.rxr[...])).astype(BF16)
+            self.z_start()
+
+        def z_start(self):
             xs, zz, (a, b) = self.xs, self.zz, self.half
             far = xs.at[(z + 4) % NZ]
             self.h = (send(far.at[every, a], zz.at[0, every, a], dz=2), send(far.at[every, b], zz.at[1, every, b], dz=6))
@@ -218,6 +229,18 @@
             wait_all(self.f)
             for k in (4, 5, 8, 9):
                 v = v + wide(self.zz[k])
+            return v
+
+    class SumLast(SumX):
+        def __init__(self):
+            self.xs, self.zz, self.half = s2, zz2, halves(COLS)
+
+        def final(self):
+            v = wide(s2[z])
+            wait_all(self.d)
+            wait_all(self.f)
+            for k in (4, 5, 8, 9):
+                v = v + wide(zz2[k])
             return v
 
     class SumZ:
@@ -337,14 +360,14 @@
 
     sums = [
         [(SumX if kind == "x" else SumZ)(refs) for (kind, _), refs in zip(SUMS[c], sum_refs[c])]
-        for c in range(CHUNKS)
+        for c in range(len(SUMS))
     ]
     spreads = [
         [
             (SpreadX if kind == "x" else SpreadZ)(refs)
             for (kind, _), refs in zip(SPREADS[c], spread_refs[c])
         ]
-        for c in range(CHUNKS)
+        for c in range(len(SPREADS))
     ]
 
     def z_first(c):
@@ -503,23 +526,80 @@
             output(c)
         return go
 
+    last, last_spread, got = SumLast(), SpreadX((p2,)), {}
+
+    def last_send(ts):
+        def go():
+            for t in ts:
+                got[t] = send_x(t)
+        return go
+
+    def last_gather(t, k):
+        b = k2 if t == 1 else v2
+
+        def go():
+            if k == 1:
+                wait_all(got[t])
+                block = b.at[0, pl.ds(0, 4), y]
+                got[t] = (send(block, block, dy=1), send(block, block, dy=3))
+            elif k == 2:
+                right, left = got[t]
+                right.wait_recv()
+                block = b.at[0, pl.ds(0, 2), (y + 3) % NY]
+                right = send(block, block, dy=1)
+                left.wait_recv()
+                block = b.at[0, pl.ds(2, 2), (y + 1) % NY]
+                got[t] = (right, send(block, block, dy=3))
+            else:
+                wait_all(got[t])
+                got[t] = [send(b.at[0], b.at[1], dc=1)]
+        return go
+
+    def last_scores():
+        wait_all(got[0])
+        wait_all(got[1])
+        for half in (0, 1):
+            r = None
+            for i in range(NX):
+                k = k2[half, i].reshape(ROWS, DEPTH)
+                d = lax.dot_general(q2[i], k, (((1,), (1,)), ((), ())), preferred_element_type=F32)
+                r = d if r is None else r + d
+            s2[:, :, pl.ds(half * ROWS, ROWS)] = (r * SCALE).astype(BF16).reshape(NZ, 16, ROWS)
+        last.z_start()
+
+    def last_soft():
+        v = last.final()
+        e = jnp.exp(v - jnp.max(v, axis=-1, keepdims=True))
+        last_spread.put((e / jnp.sum(e, axis=-1, keepdims=True)).astype(BF16))
+
+    def last_mix():
+        wait_all(last_spread.g)
+        wait_all(got[2])
+        p = last_spread.rows(x)
+        for i in range(NX):
+            m = None
+            for half in (0, 1):
+                v = v2[half, i].reshape(ROWS, DEPTH)
+                d = jnp.dot(p[:, half * ROWS : (half + 1) * ROWS], v, preferred_element_type=F32)
+                m = d if m is None else m + d
+            os_v[2, i] = m.astype(BF16)
+        ob_v[2, chip_x] = os_v[2, chip_x]
+        ms[2] = [send(os_v.at[2, (chip_x + d) % NX], ob_v.at[2, chip_x], dx=d) for d in (1, 2, 3)]
+
     schedule = [
-        first, projections(1, (1, 0)), qk_send(1), projections(2, (1, 0)), qk_send(2), projections(0, (2,)),
-        k_swap(0), score(0), k_swap(1), add(0, 1, "ring", 2), add(0, 0, "relay"), score(1),
-        add(0, 1, "ring", 3), projections(1, (2,)), k_swap(2), add(1, 1, "ring", 2), add(0, 0, "total"),
-        v_send(0), add(1, 0, "relay"), score(2), add(0, 1, "ring", 4), add(1, 1, "ring", 3),
-        add(0, 0, "relay_z"), add(2, 1, "ring", 2), add(1, 0, "total"), v_swap(0), add(0, 1, "total"),
-        add(1, 1, "ring", 4), add(2, 0, "relay"), add(2, 1, "ring", 3), add(1, 0, "relay_z"), softmax(0),
-        add(1, 1, "total"), add(2, 0, "total"), add(2, 1, "ring", 4), spread(0, 0, "pass_on"),
-        projections(2, (2,)), spread(0, 1, "gather", 1), softmax(1), add(2, 1, "total"), add(2, 0, "relay_z"),
-        spread(0, 0, "gather"), spread(0, 1, "gather", 2), spread(1, 1, "gather", 1), spread(1, 0, "pass_on"),
-        v_send(1), softmax(2), spread(1, 1, "gather", 2), v_send(2), spread(0, 1, "gather", 3),
-        spread(1, 0, "gather"), spread(0, 0, "forward"), spread(2, 1, "gather", 1), spread(2, 0, "pass_on"),
-        spread(1, 1, "gather", 3), spread(0, 1, "gather", 4), spread(2, 1, "gather", 2),
-        spread(2, 0, "gather"), v_swap(1), mix_own(0), spread(1, 1, "gather", 4), spread(2, 1, "gather", 3),
-        mix_near(0), spread(1, 0, "forward"), v_swap(2), spread(2, 1, "gather", 4), mix_own(1), mix_far(0),
-        spread(2, 0, "forward"), mix_near(1), mix_far(1), mix_own(2), mix_near(2), mix_far(2), project_out(1),
-        project_out(0), project_out(2),
+        first, projections(2, (1, 0)), projections(2, (2,)), last_send((1, 0)), projections(1, (1, 0)),
+        qk_send(1), k_swap(0), last_gather(1, 1), score(0), projections(0, (2,)), v_send(0), last_send((2,)),
+        projections(1, (2,)), k_swap(1), add(0, 1, "ring", 2), add(0, 0, "relay"), score(1),
+        add(0, 1, "ring", 3), add(1, 1, "ring", 2), last_gather(1, 2), add(0, 0, "total"), last_gather(2, 1),
+        add(1, 0, "relay"), add(0, 1, "ring", 4), add(1, 1, "ring", 3), add(0, 0, "relay_z"),
+        add(1, 0, "total"), add(0, 1, "total"), last_gather(1, 3), add(1, 1, "ring", 4), add(1, 0, "relay_z"),
+        softmax(0), add(1, 1, "total"), last_scores, spread(0, 0, "pass_on"), spread(0, 1, "gather", 1),
+        v_swap(0), last_gather(2, 2), softmax(1), last.relay_z, v_send(1), spread(1, 1, "gather", 1),
+        spread(0, 0, "gather"), last_gather(2, 3), spread(0, 1, "gather", 2), spread(1, 0, "pass_on"),
+        spread(1, 1, "gather", 2), spread(0, 1, "gather", 3), last_soft, spread(1, 0, "gather"),
+        spread(1, 1, "gather", 3), spread(0, 1, "gather", 4), spread(0, 0, "forward"), last_spread.pass_on,
+        v_swap(1), spread(1, 0, "forward"), spread(1, 1, "gather", 4), mix_own(0), mix_near(0), mix_far(0),
+        last_mix, mix_own(1), mix_near(1), mix_far(1), project_out(0), project_out(2), project_out(1),
     ]
     for step in schedule:
         step()
@@ -562,6 +642,12 @@
         pltpu.SemaphoreType.DMA((16,)),
         pltpu.SemaphoreType.DMA((N_SEMS,)),
         pltpu.SemaphoreType.DMA((N_SEMS,)),
+        V((NX, RES_LOCAL, DEPTH), BF16),
+        V((2, NX, NY, RES_LOCAL, DEPTH), BF16),
+        V((2, NX, NY, RES_LOCAL, DEPTH), BF16),
+        V((NZ, 16, COLS), BF16),
+        V((10, 16, COLS), BF16),
+        V((NX, NZ, 16, COLS), BF16),
     ]
     for table, make in ((SUMS, sum_scratch), (SPREADS, spread_scratch)):
         for row in table:

time: 79.4 us -> 73.7 us (0.928)
  Pallas kernels: 77.3 us -> 71.7 us
    pallas_call x1, Pallas kernels: 77.3 us -> 71.7 us  [body(): pl.pallas_call(kernel, out_shape=jax.ShapeDtypeStruct((rows, WIDTH), BF16...]
where the time goes in v5:
time: 73.7 us; the launch traced here: 73.6 us
  Pallas kernels  71.7 us (97%)
  matrix products  1.92 us (3%)
    pallas_call x1, Pallas kernels, body(): pl.pallas_call(kernel, out_shape=jax.ShapeDtypeStruct((rows, WIDTH), BF16...  71.7 us
    dot_general x1, matrix products, body(): out = jnp.dot(mixed, output_matrix, preferred_element_type=F32)  1.92 us

profile of v5, /device:TPU:16, one launch (start us, length us, event | category | flops | bytes accessed | tf_op | source)
XLA Modules:
  0.0 73.6 jit_solution(4921723165844822179)
XLA Ops:
  0.0 0.0 copy-start
  0.0 71.7 %shard_map.55 = bf16[512,768]{1,0:T(8,128)(2,1)S(1)} custom-call(f32[4,128,768]{2,1,0:T(8,128)} %x_hbm.1, bf16[768,768]{1,0:T(8,128)(2,1)} %wq_hbm.1, bf16[768,768]{1,0:T(8,128)(2,1)} %wk_hbm.1, bf16[768,768]{1,0:T(8,128)(2,1)} %wv_hbm.1), custom_call_target="tpu_custom_call" | custom-call | flops 5000000000 | bytes 6000000 | tf_op jit(solution)/shard_map/pallas_call | solution.py:660
  71.7 0.0 copy-done
  71.7 1.9 %fusion = f32[512,768]{1,0:T(8,128)} fusion(bf16[512,768]{1,0:T(8,128)(2,1)S(1)} %shard_map.55, bf16[768,768]{1,0:T(8,128)(2,1)S(1)} %copy-done), kind=kOutput, calls=%fused_computation | convolution fusion | flops 603979776 | bytes 3538944 | tf_op jit(solution)/shard_map/dot_general | solution.py:673
Async XLA Ops:
  0.0 71.7 %copy-start = (bf16[768,768]{1,0:T(8,128)(2,1)S(1)}, bf16[768,768]{1,0:T(8,128)(2,1)}, u32[]{:S(2)}) copy-start(bf16[768,768]{1,0:T(8,128)(2,1)} %param.9) | copy-start | bytes 3538948

commit v6 on v5

--- a/solution.py
+++ b/solution.py
@@ -26,8 +26,8 @@
     (("x", 512), ("z", 512),),
 )
 SPREADS = (
-    (("x", 512), ("z", 512),),
-    (("x", 640), ("z", 384),),
+    (("x", 768), ("z", 256),),
+    (("x", 768), ("z", 256),),
 )
 
 
@@ -587,19 +587,19 @@
         ms[2] = [send(os_v.at[2, (chip_x + d) % NX], ob_v.at[2, chip_x], dx=d) for d in (1, 2, 3)]
 
     schedule = [
-        first, projections(2, (1, 0)), projections(2, (2,)), last_send((1, 0)), projections(1, (1, 0)),
-        qk_send(1), k_swap(0), last_gather(1, 1), score(0), projections(0, (2,)), v_send(0), last_send((2,)),
-        projections(1, (2,)), k_swap(1), add(0, 1, "ring", 2), add(0, 0, "relay"), score(1),
-        add(0, 1, "ring", 3), add(1, 1, "ring", 2), last_gather(1, 2), add(0, 0, "total"), last_gather(2, 1),
-        add(1, 0, "relay"), add(0, 1, "ring", 4), add(1, 1, "ring", 3), add(0, 0, "relay_z"),
-        add(1, 0, "total"), add(0, 1, "total"), last_gather(1, 3), add(1, 1, "ring", 4), add(1, 0, "relay_z"),
-        softmax(0), add(1, 1, "total"), last_scores, spread(0, 0, "pass_on"), spread(0, 1, "gather", 1),
-        v_swap(0), last_gather(2, 2), softmax(1), last.relay_z, v_send(1), spread(1, 1, "gather", 1),
-        spread(0, 0, "gather"), last_gather(2, 3), spread(0, 1, "gather", 2), spread(1, 0, "pass_on"),
-        spread(1, 1, "gather", 2), spread(0, 1, "gather", 3), last_soft, spread(1, 0, "gather"),
-        spread(1, 1, "gather", 3), spread(0, 1, "gather", 4), spread(0, 0, "forward"), last_spread.pass_on,
-        v_swap(1), spread(1, 0, "forward"), spread(1, 1, "gather", 4), mix_own(0), mix_near(0), mix_far(0),
-        last_mix, mix_own(1), mix_near(1), mix_far(1), project_out(0), project_out(2), project_out(1),
+        first, projections(1, (1, 0)), projections(2, (1, 0)), last_send((1, 0)), projections(2, (2,)),
+        qk_send(1), k_swap(0), score(0), last_gather(1, 1), k_swap(1), add(0, 1, "ring", 2),
+        add(0, 0, "relay"), projections(1, (2,)), score(1), add(0, 1, "ring", 3), add(1, 1, "ring", 2),
+        add(1, 0, "relay"), add(0, 0, "total"), last_gather(1, 2), last_send((2,)), projections(0, (2,)),
+        add(0, 1, "ring", 4), v_send(0), add(1, 1, "ring", 3), add(0, 0, "relay_z"), add(1, 0, "total"),
+        add(0, 1, "total"), last_gather(1, 3), add(1, 1, "ring", 4), add(1, 0, "relay_z"), last_gather(2, 1),
+        softmax(0), add(1, 1, "total"), last_scores, spread(0, 1, "gather", 1), spread(0, 0, "pass_on"),
+        softmax(1), last_gather(2, 2), last.relay_z, spread(0, 0, "gather"), spread(0, 1, "gather", 2),
+        spread(1, 1, "gather", 1), spread(1, 0, "pass_on"), spread(0, 1, "gather", 3), v_send(1),
+        last_gather(2, 3), spread(1, 1, "gather", 2), last_soft, spread(1, 0, "gather"), v_swap(0),
+        spread(1, 1, "gather", 3), spread(0, 0, "forward"), spread(0, 1, "gather", 4), last_spread.pass_on,
+        v_swap(1), spread(1, 1, "gather", 4), mix_own(0), spread(1, 0, "forward"), mix_near(0), last_mix,
+        mix_far(0), mix_own(1), mix_near(1), mix_far(1), project_out(0), project_out(2), project_out(1),
     ]
     for step in schedule:
         step()

time: 73.7 us -> 72.6 us (0.985)
  Pallas kernels: 71.7 us -> 70.1 us
    pallas_call x1, Pallas kernels: 71.7 us -> 70.1 us  [body(): pl.pallas_call(kernel, out_shape=jax.ShapeDtypeStruct((rows, WIDTH), BF16...]
where the time goes in v6:
time: 72.6 us; the launch traced here: 72.1 us
  Pallas kernels  70.1 us (97%)
  matrix products  1.92 us (3%)
    pallas_call x1, Pallas kernels, body(): pl.pallas_call(kernel, out_shape=jax.ShapeDtypeStruct((rows, WIDTH), BF16...  70.1 us
    dot_general x1, matrix products, body(): out = jnp.dot(mixed, output_matrix, preferred_element_type=F32)  1.92 us

profile of v6, /device:TPU:16, one launch (start us, length us, event | category | flops | bytes accessed | tf_op | source)
XLA Modules:
  0.0 72.1 jit_solution(9911598432440738240)
XLA Ops:
  0.0 0.0 copy-start
  0.0 70.1 %shard_map.55 = bf16[512,768]{1,0:T(8,128)(2,1)S(1)} custom-call(f32[4,128,768]{2,1,0:T(8,128)} %x_hbm.1, bf16[768,768]{1,0:T(8,128)(2,1)} %wq_hbm.1, bf16[768,768]{1,0:T(8,128)(2,1)} %wk_hbm.1, bf16[768,768]{1,0:T(8,128)(2,1)} %wv_hbm.1), custom_call_target="tpu_custom_call" | custom-call | flops 5000000000 | bytes 6000000 | tf_op jit(solution)/shard_map/pallas_call | solution.py:660
  70.1 0.0 copy-done
  70.2 1.9 %fusion = f32[512,768]{1,0:T(8,128)} fusion(bf16[512,768]{1,0:T(8,128)(2,1)S(1)} %shard_map.55, bf16[768,768]{1,0:T(8,128)(2,1)S(1)} %copy-done), kind=kOutput, calls=%fused_computation | convolution fusion | flops 603979776 | bytes 3538944 | tf_op jit(solution)/shard_map/dot_general | solution.py:673
Async XLA Ops:
  0.0 70.1 %copy-start = (bf16[768,768]{1,0:T(8,128)(2,1)S(1)}, bf16[768,768]{1,0:T(8,128)(2,1)}, u32[]{:S(2)}) copy-start(bf16[768,768]{1,0:T(8,128)(2,1)} %param.9) | copy-start | bytes 3538948
